TPU v7x, 32 devices: a whole 2x2x4 slice. The times are simulated.
32 devices in a mesh: dp: 8 (over z, x), mp: 4 (over y, core).
Axes of the slice: x: 2, y: 2, z: 4, core: 2. Of those that a mesh axis runs over, the one named last changes fastest.
Arguments:
- x_lo: bfloat16 [96, 196, 768], P('dp', 'mp'), may hold values from -45 to 45
- x_hi: bfloat16 [16, 576, 768], P('dp', 'mp'), may hold values from -45 to 45
- cot_lo: bfloat16 [96, 196, 768], P('dp', 'mp'), may hold values from -6 to 6
- cot_hi: bfloat16 [16, 576, 768], P('dp', 'mp'), may hold values from -6 to 6
- counts: int32 [8, 2], P('dp'), may hold values from 1 to 12, as said below
- ln1_gain: bfloat16 [768], replicated, may hold values from 0.099609375 to 1.8984375
- ln1_bias: bfloat16 [768], replicated, may hold values from -3 to 3
- w_tok1_lo: bfloat16 [196, 384], P(None, 'mp'), may hold values from -0.4375 to 0.4375
- b_tok1_lo: bfloat16 [384], P('mp'), may hold values from -3 to 3
- w_tok2_lo: bfloat16 [384, 196], P('mp'), may hold values from -0.3125 to 0.3125
- b_tok2_lo: bfloat16 [196], P('mp'), may hold values from -3 to 3
- w_tok1_hi: bfloat16 [576, 384], P(None, 'mp'), may hold values from -0.25 to 0.25
- b_tok1_hi: bfloat16 [384], P('mp'), may hold values from -3 to 3
- w_tok2_hi: bfloat16 [384, 576], P('mp'), may hold values from -0.3125 to 0.3125
- b_tok2_hi: bfloat16 [576], P('mp'), may hold values from -3 to 3
- ln2_gain: bfloat16 [768], replicated, may hold values from 0.099609375 to 1.8984375
- ln2_bias: bfloat16 [768], replicated, may hold values from -3 to 3
- w_chan_in: bfloat16 [768, 3072], replicated, may hold values from -0.21875 to 0.21875
- b_chan_in: bfloat16 [3072], replicated, may hold values from -3 to 3
- w_chan_out: bfloat16 [3072, 768], replicated, may hold values from -0.109375 to 0.109375
- b_chan_out: bfloat16 [768], replicated, may hold values from -3 to 3
Outputs:
- out_lo: bfloat16 [96, 196, 768], P('dp', 'mp')
- out_hi: bfloat16 [16, 576, 768], P('dp', 'mp')
- grad_lo: float32 [96, 196, 768], P('dp', 'mp')
- grad_hi: float32 [16, 576, 768], P('dp', 'mp')
- g_ln1_gain: float32 [768], replicated
- g_ln1_bias: float32 [768], replicated
- g_w_tok1_lo: float32 [196, 384], P(None, 'mp')
- g_b_tok1_lo: float32 [384], P('mp')
- g_w_tok2_lo: float32 [384, 196], P('mp')
- g_b_tok2_lo: float32 [196], P('mp')
- g_w_tok1_hi: float32 [576, 384], P(None, 'mp')
- g_b_tok1_hi: float32 [384], P('mp')
- g_w_tok2_hi: float32 [384, 576], P('mp')
- g_b_tok2_hi: float32 [576], P('mp')
- g_ln2_gain: float32 [768], replicated
- g_ln2_bias: float32 [768], replicated
- g_w_chan_in: float32 [768, 3072], replicated
- g_b_chan_in: float32 [3072], replicated
- g_w_chan_out: float32 [3072, 768], replicated
- g_b_chan_out: float32 [768], replicated
Inputs may be any that keep to these rules, and one draw needn't show every extreme that they name: counts[g, 0] is at most 12 and counts[g, 1] at most 2; some group has all its 224 px slots live and some group all its 384 px slots.
All inputs are finite; a program needn't handle non-finite values.
Results may differ from a plain program's by a relative error of at most 0.0071.
Values may be sent and summed in bfloat16 or wider, within the bound.
A program may use at most 192 MiB of HBM per device.

v0:
```python
import jax
import jax.numpy as jnp
from jax import lax
from jax.sharding import PartitionSpec as P

EPS = 1e-06


def normalize(values, ln_gain, ln_shift):
    centre = values - jnp.mean(values, axis=-1, keepdims=True)
    spread = jnp.mean(centre * centre, axis=-1, keepdims=True)
    return centre * lax.rsqrt(spread + EPS) * ln_gain + ln_shift


def token_forward(normed, w_in, b_in, w_out):
    pre_token = (
        jnp.einsum("npd,pk->nkd", normed, w_in, preferred_element_type=jnp.float32)
        + b_in.astype(jnp.float32)[None, :, None]
    )
    hid_token = jax.nn.gelu(pre_token).astype(jnp.bfloat16)
    return jnp.einsum("nkd,kp->npd", hid_token, w_out, preferred_element_type=jnp.float32)


def token_backward(normed, grad_mix, w_in, b_in, w_out):
    pre_token = (
        jnp.einsum("npd,pk->nkd", normed, w_in, preferred_element_type=jnp.float32)
        + b_in.astype(jnp.float32)[None, :, None]
    )
    hid_act, gelu_pull = jax.vjp(jax.nn.gelu, pre_token)
    hid_token = hid_act.astype(jnp.bfloat16)
    grad_w_out = jnp.einsum("nkd,npd->kp", hid_token, grad_mix, preferred_element_type=jnp.float32)
    grad_hid = jnp.einsum("kp,npd->nkd", w_out, grad_mix, preferred_element_type=jnp.float32)
    grad_pre = gelu_pull(grad_hid)[0].astype(jnp.bfloat16)
    grad_b_in = jnp.sum(grad_pre, axis=(0, 2), dtype=jnp.float32)
    grad_w_in = jnp.einsum("npd,nkd->pk", normed, grad_pre, preferred_element_type=jnp.float32)
    grad_normed = jnp.einsum("pk,nkd->npd", w_in, grad_pre, preferred_element_type=jnp.float32)
    return (grad_normed, grad_w_in, grad_b_in, grad_w_out)


def channel_forward(stream, gain_two, shift_two, w_chan_in, b_chan_in, w_chan_out, b_chan_out):
    normed_two = normalize(stream, gain_two, shift_two).astype(jnp.bfloat16)
    pre_chan = jnp.dot(
        normed_two, w_chan_in, preferred_element_type=jnp.float32
    ) + b_chan_in.astype(jnp.float32)
    hid_chan = jax.nn.gelu(pre_chan).astype(jnp.bfloat16)
    return (
        stream
        + jnp.dot(hid_chan, w_chan_out, preferred_element_type=jnp.float32)
        + b_chan_out.astype(jnp.float32)
    )


def channel_backward(stream, grad_out, gain_two, shift_two, w_chan_in, b_chan_in, w_chan_out):
    normed_f, ln_pull = jax.vjp(normalize, stream, gain_two, shift_two)
    normed_two = normed_f.astype(jnp.bfloat16)
    pre_chan = jnp.dot(
        normed_two, w_chan_in, preferred_element_type=jnp.float32
    ) + b_chan_in.astype(jnp.float32)
    hid_act, gelu_pull = jax.vjp(jax.nn.gelu, pre_chan)
    hid_chan = hid_act.astype(jnp.bfloat16)
    grad_bf = grad_out.astype(jnp.bfloat16)
    grad_w_out = jnp.einsum("rf,rd->fd", hid_chan, grad_bf, preferred_element_type=jnp.float32)
    grad_b_out = jnp.sum(grad_out, axis=0)
    grad_hid = jnp.einsum("rd,fd->rf", grad_bf, w_chan_out, preferred_element_type=jnp.float32)
    grad_pre = gelu_pull(grad_hid)[0].astype(jnp.bfloat16)
    grad_w_in = jnp.einsum("rd,rf->df", normed_two, grad_pre, preferred_element_type=jnp.float32)
    grad_b_in = jnp.sum(grad_pre, axis=0, dtype=jnp.float32)
    grad_normed = jnp.einsum("rf,df->rd", grad_pre, w_chan_in, preferred_element_type=jnp.float32)
    grad_stream, grad_gain, grad_shift = ln_pull(grad_normed)
    return (
        grad_out + grad_stream,
        grad_w_in,
        grad_b_in,
        grad_w_out,
        grad_b_out,
        grad_gain,
        grad_shift,
    )


def body(
    x_lo,
    x_hi,
    cot_lo,
    cot_hi,
    counts,
    ln1_gain,
    ln1_bias,
    w_tok1_lo,
    b_tok1_lo,
    w_tok2_lo,
    b_tok2_lo,
    w_tok1_hi,
    b_tok1_hi,
    w_tok2_hi,
    b_tok2_hi,
    ln2_gain,
    ln2_bias,
    w_chan_in,
    b_chan_in,
    w_chan_out,
    b_chan_out,
):
    slots_lo, rows_lo, model_width = x_lo.shape
    slots_hi, rows_hi = (x_hi.shape[0], x_hi.shape[1])
    split_at = slots_lo * rows_lo
    live_lo = (jnp.arange(slots_lo) < counts[0, 0]).astype(jnp.float32)[:, None, None]
    live_hi = (jnp.arange(slots_hi) < counts[0, 1]).astype(jnp.float32)[:, None, None]
    gain_one = ln1_gain.astype(jnp.float32)
    shift_one = ln1_bias.astype(jnp.float32)
    gain_two = ln2_gain.astype(jnp.float32)
    shift_two = ln2_bias.astype(jnp.float32)
    input_lo = x_lo.astype(jnp.float32)
    input_hi = x_hi.astype(jnp.float32)
    stream = jnp.concatenate(
        [input_lo.reshape(-1, model_width), input_hi.reshape(-1, model_width)], axis=0
    )
    normed_f, ln1_pull = jax.vjp(normalize, stream, gain_one, shift_one)
    normed = normed_f.astype(jnp.bfloat16)
    normed_lo = normed[:split_at].reshape(slots_lo, rows_lo, model_width)
    normed_hi = normed[split_at:].reshape(slots_hi, rows_hi, model_width)
    w_in_lo, w_in_hi, b_in_lo, b_in_hi, w_out_lo, w_out_hi = (
        w_tok1_lo,
        w_tok1_hi,
        b_tok1_lo,
        b_tok1_hi,
        w_tok2_lo,
        w_tok2_hi,
    )
    full_lo, full_hi = (
        lax.all_gather(normed_lo, "mp", axis=1, tiled=True),
        lax.all_gather(normed_hi, "mp", axis=1, tiled=True),
    )
    part_lo = token_forward(full_lo, w_in_lo, b_in_lo, w_out_lo)
    part_hi = token_forward(full_hi, w_in_hi, b_in_hi, w_out_hi)
    mix_lo, mix_hi = (
        lax.psum_scatter(part_lo, "mp", scatter_dimension=1, tiled=True),
        lax.psum_scatter(part_hi, "mp", scatter_dimension=1, tiled=True),
    )
    after_lo = input_lo + mix_lo + b_tok2_lo.astype(jnp.float32)[None, :, None]
    after_hi = input_hi + mix_hi + b_tok2_hi.astype(jnp.float32)[None, :, None]
    after_token = jnp.concatenate(
        [after_lo.reshape(-1, model_width), after_hi.reshape(-1, model_width)], axis=0
    )
    chan_out = channel_forward(
        after_token, gain_two, shift_two, w_chan_in, b_chan_in, w_chan_out, b_chan_out
    )
    out_lo = (chan_out[:split_at].reshape(slots_lo, rows_lo, model_width) * live_lo).astype(
        jnp.bfloat16
    )
    out_hi = (chan_out[split_at:].reshape(slots_hi, rows_hi, model_width) * live_hi).astype(
        jnp.bfloat16
    )
    grad_out = jnp.concatenate(
        [
            (cot_lo.astype(jnp.float32) * live_lo).reshape(-1, model_width),
            (cot_hi.astype(jnp.float32) * live_hi).reshape(-1, model_width),
        ],
        axis=0,
    )
    grad_after, grad_wc_in, grad_bc_in, grad_wc_out, grad_bc_out, grad_gain_two, grad_shift_two = (
        channel_backward(
            after_token, grad_out, gain_two, shift_two, w_chan_in, b_chan_in, w_chan_out
        )
    )
    mix_grad = grad_after.astype(jnp.bfloat16)
    mix_grad_lo = mix_grad[:split_at].reshape(slots_lo, rows_lo, model_width)
    mix_grad_hi = mix_grad[split_at:].reshape(slots_hi, rows_hi, model_width)
    grad_bias_lo = jnp.sum(mix_grad_lo, axis=(0, 2), dtype=jnp.float32)
    grad_bias_hi = jnp.sum(mix_grad_hi, axis=(0, 2), dtype=jnp.float32)
    grad_full_lo, grad_full_hi = (
        lax.all_gather(mix_grad_lo, "mp", axis=1, tiled=True),
        lax.all_gather(mix_grad_hi, "mp", axis=1, tiled=True),
    )
    back_lo = token_backward(full_lo, grad_full_lo, w_in_lo, b_in_lo, w_out_lo)
    back_hi = token_backward(full_hi, grad_full_hi, w_in_hi, b_in_hi, w_out_hi)
    normed_grad_lo, normed_grad_hi = (
        lax.psum_scatter(back_lo[0], "mp", scatter_dimension=1, tiled=True),
        lax.psum_scatter(back_hi[0], "mp", scatter_dimension=1, tiled=True),
    )
    token_parts = (back_lo[1], back_lo[2], back_lo[3], back_hi[1], back_hi[2], back_hi[3])
    grad_normed = jnp.concatenate(
        [normed_grad_lo.reshape(-1, model_width), normed_grad_hi.reshape(-1, model_width)], axis=0
    )
    grad_ln_stream, grad_gain_one, grad_shift_one = ln1_pull(grad_normed)
    grad_stream = grad_after + grad_ln_stream
    grad_lo = grad_stream[:split_at].reshape(slots_lo, rows_lo, model_width)
    grad_hi = grad_stream[split_at:].reshape(slots_hi, rows_hi, model_width)
    dense_total = lax.psum(
        (
            grad_gain_one,
            grad_shift_one,
            grad_gain_two,
            grad_shift_two,
            grad_wc_in,
            grad_bc_in,
            grad_wc_out,
            grad_bc_out,
        ),
        ("dp", "mp"),
    )
    token_total = lax.psum(
        (
            token_parts[0],
            token_parts[1],
            token_parts[2],
            grad_bias_lo,
            token_parts[3],
            token_parts[4],
            token_parts[5],
            grad_bias_hi,
        ),
        "dp",
    )
    return (
        out_lo,
        out_hi,
        grad_lo,
        grad_hi,
        dense_total[0],
        dense_total[1],
        token_total[0],
        token_total[1],
        token_total[2],
        token_total[3],
        token_total[4],
        token_total[5],
        token_total[6],
        token_total[7],
        dense_total[2],
        dense_total[3],
        dense_total[4],
        dense_total[5],
        dense_total[6],
        dense_total[7],
    )


def solution(mesh):
    return jax.shard_map(
        body,
        mesh=mesh,
        in_specs=(
            P("dp", "mp", None),
            P("dp", "mp", None),
            P("dp", "mp", None),
            P("dp", "mp", None),
            P("dp", None),
            P(),
            P(),
            P(None, "mp"),
            P("mp"),
            P("mp", None),
            P("mp"),
            P(None, "mp"),
            P("mp"),
            P("mp", None),
            P("mp"),
            P(),
            P(),
            P(),
            P(),
            P(),
            P(),
        ),
        out_specs=(
            P("dp", "mp", None),
            P("dp", "mp", None),
            P("dp", "mp", None),
            P("dp", "mp", None),
            P(),
            P(),
            P(None, "mp"),
            P("mp"),
            P("mp", None),
            P("mp"),
            P(None, "mp"),
            P("mp"),
            P("mp", None),
            P("mp"),
            P(),
            P(),
            P(),
            P(),
            P(),
            P(),
        ),
        check_vma=False,
    )
```

profile of v0, /device:TPU:0, one launch (start us, length us, event | category | flops | bytes accessed | tf_op | source)
XLA Modules:
  0.0 996.4 jit_solution(5821603523559467599)
XLA Ops:
  21.9 38.8 %all-gather.5.cloned.1.call-done = bf16[12,196,768]{2,0,1:T(8,128)(2,1)} async-done(((bf16[12,49,768]{2,0,1:T(8,128)(2,1)}), bf16[12,196,768]{2,0,1:T(8,128)(2,1)}) %all-gather.5.cloned.1.call-update) | async-done | bytes 3612688 | tf_op jit(solution)/shard_map/all_gather | solution.py:131
  66.3 4.8 convolution_bitcast_fusion.1
  71.7 11.9 %all-gather.7.cloned.1.call-done = bf16[2,576,768]{2,1,0:T(8,128)(2,1)} async-done(((bf16[2,144,768]{2,1,0:T(8,128)(2,1)}), bf16[2,576,768]{2,1,0:T(8,128)(2,1)}) %all-gather.7.cloned.1.call-update) | async-done | bytes 1769488 | tf_op jit(solution)/shard_map/all_gather | solution.py:132
  100.7 123.1 %all-reduce.11.cloned.1.call-done = f32[12,196,768]{2,1,0:T(8,128)} async-done(((f32[12,196,768]{2,1,0:T(8,128)}), f32[12,196,768]{2,1,0:T(8,128)}) %all-reduce.11.cloned.1.call-update) | async-done | bytes 7225360
  230.2 37.3 %reduce-scatter.5.cloned.1.call-done = f32[2,144,768]{2,1,0:T(8,128)} async-done(((f32[2,576,768]{2,1,0:T(8,128)}), f32[2,144,768]{2,1,0:T(8,128)}) %reduce-scatter.5.cloned.1.call-update) | async-done | bytes 884752 | tf_op jit(solution)/shard_map/reduce_scatter | solution.py:138
  271.4 6.6 fusion.70
  278.1 6.7 add_add_fusion.4
  289.9 4.6 fusion.66
  300.2 16.1 %convert_reduce_fusion = (f32[3072]{0:T(1024)}, bf16[876,3072]{1,0:T(8,128)(2,1)S(1)}) fusion(f32[876,3072]{1,0:T(8,128)} %copy-done.59, f32[3072]{0:T(1024)} %convert_element_type.130, bf16[3072,768]{1,0:T(8,128)(2,1)} %param.40, f32[288,768]{1,0:T(8,128)S(1)} %bitcast.116, f32[588,768]{1,0:T(8,128)} %reshape.179), kind=kOutput, calls=%fused_computation.9 | convolution fusion | flops 4198069248 | bytes 23580672 | tf_op jit(solution)/shard_map/rd,fd->rf/dot_general | solution.py:64
  316.3 9.8 multiply_reduce_fusion
  337.6 36.0 %all-gather.9.cloned.1.call-done = bf16[12,196,768]{2,0,1:T(8,128)(2,1)} async-done(((bf16[12,49,768]{2,0,1:T(8,128)(2,1)}), bf16[12,196,768]{2,0,1:T(8,128)(2,1)}) %all-gather.9.cloned.1.call-update) | async-done | bytes 3612688 | tf_op jit(solution)/shard_map/all_gather | solution.py:172
  373.6 7.7 convert_reduce_fusion.1
  386.7 9.8 all-gather.11.cloned.1.call-done
  403.1 14.7 %fusion.46 = f32[3072,768]{1,0:T(8,128)} fusion(f32[288,768]{1,0:T(8,128)} %bitcast.118, f32[588,768]{1,0:T(8,128)} %reshape.179, f32[876,3072]{1,0:T(8,128)} %copy-done.59, f32[3072]{0:T(1024)S(1)} %copy-done.42), kind=kOutput, calls=%fused_computation.87 | convolution fusion | flops 4163088384 | bytes 22904832 | tf_op jit(solution)/shard_map/rf,rd->fd/dot_general | solution.py:62
  420.7 5.5 fusion.33
  426.1 5.8 fusion.36
  432.3 10.6 %fusion.69 = f32[768,3072]{1,0:T(8,128)} fusion(bf16[876,3072]{1,0:T(8,128)(2,1)} %copy-done.58, f32[768]{0:T(1024)S(1)} %copy-done.45, f32[768]{0:T(1024)S(1)} %copy-done.35, f32[876]{0:T(1024)S(1)} %copy-done.38, f32[876]{0:T(1024)S(1)} %broadcast_multiply_fusion, f32[288,768]{1,0:T(8,128)} %bitcast.108, f32[588,768]{1,0:T(8,128)} %reshape.174), kind=kOutput, calls=%fused_computation.117 | convolution fusion | flops 4137523200 | bytes 17523552 | tf_op jit(solution)/shard_map/rd,rf->df/dot_general | solution.py:66
  445.9 21.9 %all-reduce.4 = (f32[96]{0:T(128)}, f32[49]{0:T(128)}, f32[96]{0:T(128)}, f32[144]{0:T(256)}) all-reduce(f32[96]{0:T(128)S(1)} %copy-done.53, f32[49]{0:T(128)S(1)} %reduce_sum.247, f32[96]{0:T(128)S(1)} %copy-done.54, f32[144]{0:T(256)S(1)} %reduce_sum.251), channel_id=1, replica_groups=mesh['dp'=8,'mp'=4] {'dp'}, use_global_device_ids=true, to_apply=%region_19.0 | all-reduce | flops 385 | bytes 3080 | tf_op jit(solution)/shard_map/psum | solution.py:202
  467.8 68.4 %all-reduce.13.cloned.1.call-done = f32[12,196,768]{2,1,0:T(8,128)} async-done(((f32[12,196,768]{2,1,0:T(8,128)}), f32[12,196,768]{2,1,0:T(8,128)}) %all-reduce.13.cloned.1.call-update) | async-done | bytes 7225360
  542.2 37.4 %reduce-scatter.7.cloned.1.call-done = f32[2,144,768]{2,1,0:T(8,128)} async-done(((f32[2,576,768]{2,1,0:T(8,128)}), f32[2,144,768]{2,1,0:T(8,128)}) %reduce-scatter.7.cloned.1.call-update) | async-done | bytes 884752 | tf_op jit(solution)/shard_map/reduce_scatter | solution.py:179
  590.6 40.6 %all-reduce.2 = (f32[768]{0:T(1024)}, f32[768]{0:T(1024)}, f32[768]{0:T(1024)}, f32[768]{0:T(1024)}, f32[3072]{0:T(1024)}, /*index=5*/f32[768]{0:T(1024)}) all-reduce(f32[768]{0:T(1024)S(1)} %get-tuple-element.20, f32[768]{0:T(1024)S(1)} %reduce_sum.243, f32[768]{0:T(1024)S(1)} %copy-done.47, ...), channel_id=1, replica_groups=mesh['dp'=8,'mp'=4] {'dp','mp'}, use_global_device_ids=true, to_apply=%region_13.0 | all-reduce | flops 6912 | bytes 55296 | tf_op jit(solution)/shard_map/psum | solution.py:189
  631.2 28.1 %all-reduce.17.cloned.1.call-done = (f32[196,96]{0,1:T(8,128)}, f32[96,196]{1,0:T(8,128)}, f32[576,96]{0,1:T(8,128)}, f32[96,576]{1,0:T(8,128)}) async-done(((f32[196,96]{0,1:T(8,128)}, f32[96,196]{1,0:T(8,128)}, f32[576,96]{0,1:T(8,128)}, f32[96,576]{1,0:T(8,128)}), (f32[196,96]{0,1:T(8,128)}, f32[96,196]{1,0:T(8,128)}, f32[576,96]{0,1:T(8,128)}, f32[96,576]{1,0:T(8,128)})) %all-reduce.17.cloned.1.call-update) | async-done | bytes 592912 | tf_op jit(solution)/shard_map/psum | solution.py:202
  659.3 311.0 %all-reduce.15.cloned.1.call-done = (f32[768,3072]{1,0:T(8,128)}, f32[3072,768]{1,0:T(8,128)}) async-done(((f32[768,3072]{1,0:T(8,128)}, f32[3072,768]{1,0:T(8,128)}), (f32[768,3072]{1,0:T(8,128)}, f32[3072,768]{1,0:T(8,128)})) %all-reduce.15.cloned.1.call-update) | async-done | bytes 18874384 | tf_op jit(solution)/shard_map/psum | solution.py:189
  976.8 8.8 copy.85
  (229 shorter events, 114.7 us)
Async XLA Ops:
  7.2 78.4 %copy-start = (bf16[96,576]{1,0:T(8,128)(2,1)S(1)}, bf16[96,576]{1,0:T(8,128)(2,1)}, u32[]{:S(2)}) copy-start(bf16[96,576]{1,0:T(8,128)(2,1)} %param.34) | copy-start | bytes 331780
  7.2 53.5 %all-gather.5.cloned.1.call-start = ((), (), s32[]{:S(2)}) async-start(), calls=%async_computation.2 | async-start | bytes 6021120 | tf_op jit(solution)/shard_map/all_gather | solution.py:131
  17.4 43.3 %copy-start.24 = (bf16[196,96]{0,1:T(8,128)(2,1)S(1)}, bf16[196,96]{0,1:T(8,128)(2,1)}, u32[]{:S(2)}) copy-start(bf16[196,96]{0,1:T(8,128)(2,1)} %param.28) | copy-start | bytes 112900
  19.8 63.8 %all-gather.7.cloned.1.call-start = ((), (), s32[]{:S(2)}) async-start(), calls=%async_computation.3 | async-start | bytes 2211840 | tf_op jit(solution)/shard_map/all_gather | solution.py:132
  21.8 202.0 %all-reduce.11.cloned.1.call-start = ((), (), s32[]{:S(2)}) async-start(), calls=%async_computation.8 | async-start | bytes 14745600
  21.9 42.6 %copy-start.51 = (f32[96]{0:T(128)}, f32[96]{0:T(128)S(1)}, u32[]{:S(2)}) copy-start(f32[96]{0:T(128)S(1)} %convert_element_type.121) | copy-start | bytes 1156
  21.9 44.4 %copy-start.26 = (bf16[96,196]{1,0:T(8,128)(2,1)S(1)}, bf16[96,196]{1,0:T(8,128)(2,1)}, u32[]{:S(2)}) copy-start(bf16[96,196]{1,0:T(8,128)(2,1)} %param.30) | copy-start | bytes 112900
  71.1 12.6 %copy-start.23 = (bf16[576,96]{0,1:T(8,128)(2,1)S(1)}, bf16[576,96]{0,1:T(8,128)(2,1)}, u32[]{:S(2)}) copy-start(bf16[576,96]{0,1:T(8,128)(2,1)} %param.32) | copy-start | bytes 331780
  71.1 196.4 %reduce-scatter.5.cloned.1.call-start = ((), (), s32[]{:S(2)}) async-start(), calls=%async_computation.4 | async-start | bytes 4423680 | tf_op jit(solution)/shard_map/reduce_scatter | solution.py:138
  88.1 285.5 %all-gather.9.cloned.1.call-start = ((), (), s32[]{:S(2)}) async-start(), calls=%async_computation.5 | async-start | bytes 6021120 | tf_op jit(solution)/shard_map/all_gather | solution.py:172
  227.4 40.1 %copy-start.50 = (f32[144]{0:T(256)S(1)}, f32[144]{0:T(256)}, u32[]{:S(2)}) copy-start(f32[144]{0:T(256)} %convert_element_type.126) | copy-start | bytes 1732
  300.1 27.1 %copy-start.15 = (f32[2,144,768]{2,1,0:T(8,128)}, f32[2,144,768]{2,1,0:T(8,128)S(1)}, u32[]{:S(2)}) copy-start(f32[2,144,768]{2,1,0:T(8,128)S(1)} %get-tuple-element.48) | copy-start | bytes 2654212
  300.1 16.1 %copy-start.2 = (f32[588,768]{1,0:T(8,128)S(1)}, f32[588,768]{1,0:T(8,128)}, u32[]{:S(2)}) copy-start(f32[588,768]{1,0:T(8,128)} %reshape.174) | copy-start | bytes 5419012
  300.1 16.1 %copy-start.11 = (f32[2,144,768]{2,1,0:T(8,128)S(1)}, f32[2,144,768]{2,1,0:T(8,128)}, u32[]{:S(2)}) copy-start(f32[2,144,768]{2,1,0:T(8,128)} %copy-done.10) | copy-start | bytes 2654212
  300.1 16.1 %copy-start.34 = (f32[768]{0:T(1024)S(1)}, f32[768]{0:T(1024)}, u32[]{:S(2)}) copy-start(f32[768]{0:T(1024)} %convert_element_type.127) | copy-start | bytes 9220
  300.1 16.1 %copy-start.37 = (f32[876]{0:T(1024)S(1)}, f32[876]{0:T(1024)}, u32[]{:S(2)}) copy-start(f32[876]{0:T(1024)} %copy-done.36) | copy-start | bytes 10516
  335.5 61.0 %all-gather.11.cloned.1.call-start = ((), (), s32[]{:S(2)}) async-start(), calls=%async_computation.6 | async-start | bytes 2211840 | tf_op jit(solution)/shard_map/all_gather | solution.py:173
  337.4 198.8 %all-reduce.13.cloned.1.call-start = ((), (), s32[]{:S(2)}) async-start(), calls=%async_computation.9 | async-start | bytes 14745600
  386.7 193.0 %reduce-scatter.7.cloned.1.call-start = ((), (), s32[]{:S(2)}) async-start(), calls=%async_computation.7 | async-start | bytes 4423680 | tf_op jit(solution)/shard_map/reduce_scatter | solution.py:179
  402.5 256.8 %all-reduce.17.cloned.1.call-start = ((), (), s32[]{:S(2)}) async-start(), calls=%async_computation.11 | async-start | bytes 1376256 | tf_op jit(solution)/shard_map/psum | solution.py:202
  403.1 14.7 %copy-start.17 = (bf16[2,576,768]{2,1,0:T(8,128)(2,1)S(1)}, bf16[2,576,768]{2,1,0:T(8,128)(2,1)}, u32[]{:S(2)}) copy-start(bf16[2,576,768]{2,1,0:T(8,128)(2,1)} %all-gather.7.cloned.1.call-done) | copy-start | bytes 5308420
  403.1 14.7 %copy-start.22 = (bf16[2,96,768]{2,1,0:T(8,128)(2,1)S(1)}, bf16[2,96,768]{2,1,0:T(8,128)(2,1)}, u32[]{:S(2)}) copy-start(bf16[2,96,768]{2,1,0:T(8,128)(2,1)} %copy-done.21) | copy-start | bytes 884740
  403.1 16.1 %copy-start.55 = (bf16[2,576,768]{2,1,0:T(8,128)(2,1)S(1)}, bf16[2,576,768]{2,1,0:T(8,128)(2,1)}, u32[]{:S(2)}) copy-start(bf16[2,576,768]{2,1,0:T(8,128)(2,1)} %all-gather.11.cloned.1.call-done) | copy-start | bytes 5308420
  432.0 538.3 %all-reduce.15.cloned.1.call-start = ((), (), s32[]{:S(2)}) async-start(), calls=%async_computation.10 | async-start | bytes 37748736 | tf_op jit(solution)/shard_map/psum | solution.py:189
  (51 other events, 195.0 us)
Sparse Core Ops, SparseCore 0:
  20.0 40.7 all-gather.4
  62.8 20.7 all-gather.6
  86.6 137.1 all-reduce.10
  226.8 40.6 reduce-scatter.4
  335.6 38.0 all-gather.8
  375.7 20.7 all-gather.10
  399.0 137.1 all-reduce.12
  538.9 40.6 reduce-scatter.6
  584.6 74.5 all-reduce.16
  667.2 303.0 all-reduce.14
where the time goes:
time: 1000 us; the launch traced here: 996 us
  waiting for transfers between devices  702 us (70%)
  matrix products  109 us (11%)
  local copies, waits for them, and re-layouts  65.8 us (7%)
  blocking collectives  62.5 us (6%)
  other arithmetic  40.9 us (4%)
  between operations  15.7 us (2%)
    psum x1, waiting for transfers between devices, body(): lax.psum((grad_gain_one, grad_shift_one, grad_gain_two, grad_shift_two, g...  311 us
    unnamed x12, waiting for transfers between devices  192 us
    psum x1, blocking collectives, body(): lax.psum((grad_gain_one, grad_shift_one, grad_gain_two, grad_shift_two, g...  40.6 us
    all_gather x1, waiting for transfers between devices, body(): lax.all_gather(normed_lo, 'mp', axis=1, tiled=True)  38.8 us
    reduce_scatter x1, waiting for transfers between devices, body(): lax.psum_scatter(back_hi[0], 'mp', scatter_dimension=1, tiled=True)  37.4 us
    reduce_scatter x1, waiting for transfers between devices, body(): lax.psum_scatter(part_hi, 'mp', scatter_dimension=1, tiled=True)  37.3 us
    all_gather x1, waiting for transfers between devices, body(): lax.all_gather(mix_grad_lo, 'mp', axis=1, tiled=True)  36 us
    unnamed x137, local copies, waits for them, and re-layouts  31.9 us
  transfers between devices with their start and end apart: 10, of which 10 were waited for; matrix products, arithmetic and copies ran while one was open for 11% of the time, Pallas kernels for 0%

commit v1 on v0

v1 whole, which is shorter than its diff:
```python
import functools

import jax
import jax.numpy as jnp
from jax import lax
from jax.experimental import pallas as pl
from jax.experimental.pallas import tpu as pltpu
from jax.sharding import PartitionSpec as P

MESH = pl.DeviceIdType.MESH
EPS = 1e-06
GELU_A, GELU_B = 0.7978845608028654, 0.044715
f32, bf16 = jnp.float32, jnp.bfloat16

LINE, PAIR = 4, 2
SHARDS = 16
LAND = {"xzy": dict(x=(0, 8), z=(8, 10), y=(18, 1)),
        "yzx": dict(y=(0, 8), z=(8, 10), x=(18, 1))}
LANDED = 19
NSEM = 10


class Place:
    def __init__(self):
        dp, mp = lax.axis_index("dp"), lax.axis_index("mp")
        self.block = dp // (LINE * PAIR)
        self.z = (dp // PAIR) % LINE
        self.x = dp % PAIR
        self.y = mp // 2
        self.c = mp % 2

    def at(self, z=None, x=None, y=None, c=None):
        z = self.z if z is None else z
        x = self.x if x is None else x
        y = self.y if y is None else y
        c = self.c if c is None else c
        return (self.block * (LINE * PAIR) + z * PAIR + x, y * 2 + c)

    def up(self):
        return self.at(z=jnp.minimum(self.z + 1, LINE - 1))

    def down(self):
        return self.at(z=jnp.maximum(self.z - 1, 0))

    def pair(self, axis):
        return self.at(**{axis: 1 - getattr(self, axis)})


def add_into(ref, idx, *others):
    total = ref[idx].astype(f32)
    for o in others:
        total = total + o.astype(f32)
    ref[idx] = total.astype(bf16)


class AllReduce:
    def __init__(self, place, g, land_core, land, out, send, recv, kept):
        self.p, self.g, self.lc, self.l, self.out, self.send, self.recv, self.kept = place, g, land_core, land, out, send, recv, kept
        self.unit = g.shape[1] // (2 * SHARDS)

    def sh(self, start, n):
        if isinstance(start, int):
            return pl.ds(start * self.unit, n * self.unit)
        return pl.ds(pl.multiple_of(start * self.unit, 16), n * self.unit)

    def copy(self, f, k, src, dst, dev):
        return pltpu.make_async_remote_copy(src, dst, self.send.at[f, k], self.recv.at[f, k], device_id=dev, device_id_type=MESH)

    def half(self, f, start, n):
        return self.g.at[f, self.sh(self.p.c * SHARDS + start, n)]

    def core(self, f):
        p = self.p
        return [self.copy(f, 0, self.g.at[f, self.sh((1 - p.c) * SHARDS, SHARDS)], self.lc.at[f % self.lc.shape[0]], p.pair("c"))]

    def core_add(self, f):
        add_into(self.g, (f, self.sh(self.p.c * SHARDS, SHARDS)), self.lc[f % self.lc.shape[0]])

    def regions(self, path):
        base, n, out = 0, SHARDS, {}
        for axis in path:
            out[axis] = (base, n)
            parts = LINE if axis == "z" else PAIR
            n = n // parts
            base = base + getattr(self.p, axis) * n
        out["end"] = (base, n)
        return out

    def pair_send(self, f, path, axis):
        base, n = self.regions(path)[axis]
        other = 1 - getattr(self.p, axis)
        off, m = LAND[path][axis]
        k = {"x": 1, "y": 2}[axis]
        return [self.copy(f, k, self.half(f, base + other * (n // 2), n // 2), self.l.at[f, self.sh(off, m)], self.p.pair(axis))]

    def pair_add(self, f, path, axis):
        base, n = self.regions(path)[axis]
        off, m = LAND[path][axis]
        s = self.p.c * SHARDS + base + getattr(self.p, axis) * m
        add_into(self.g, (f, self.sh(s, m)), self.l[f, self.sh(off, m)])

    def z_copies(self, f, path, k, back):
        base, n = self.regions(path)["z"]
        m = n // LINE
        off, _ = LAND[path]["z"]
        z = self.p.z
        if back:
            up, down = self.done(f, base, k * m), self.done(f, base + (LINE - k) * m, k * m)
            up = self.copy(f, 7, up, up, self.p.up())
            down = self.copy(f, 8, down, down, self.p.down())
        else:
            w = (LINE - k) * m
            up = self.copy(f, 3, self.half(f, base + k * m, w), self.l.at[f, self.sh(off, w)], self.p.up())
            down = self.copy(f, 4, self.half(f, base, w), self.l.at[f, self.sh(off + (k + 1) * m, w)], self.p.down())
        return [(z == k - 1, z == k, up), (z == LINE - k, z == LINE - 1 - k, down)]

    def z_add(self, f, path, k):
        base, n = self.regions(path)["z"]
        m = n // LINE
        off, _ = LAND[path]["z"]
        c0 = self.p.c * SHARDS + base
        w = (LINE - k) * m

        @pl.when(self.p.z == k)
        def _():
            add_into(self.g, (f, self.sh(c0 + k * m, w)), self.l[f, self.sh(off, w)])

        @pl.when(self.p.z == LINE - 1 - k)
        def _():
            add_into(self.g, (f, self.sh(c0, w)), self.l[f, self.sh(off + (k + 1) * m, w)])

    def done(self, f, start, n):
        return self.out.at[f, self.sh(self.p.c * SHARDS + start, n)]

    def same(self, f, k, start, n, dev):
        ref = self.done(f, start, n)
        return self.copy(f, k, ref, ref, dev)

    def pair_back(self, f, path, axis):
        base, n = self.regions(path)[axis]
        k = {"x": 5, "y": 6}[axis]
        if axis == path[-1]:
            at, ref = self.regions(path)["end"]
            src, dst = self.half(f, at, ref), self.done(f, at, ref)
            return [self.copy(f, k, src, dst, self.p.pair(axis)), pltpu.make_async_copy(src, dst, self.kept.at[f])]
        return [self.same(f, k, base + getattr(self.p, axis) * (n // 2), n // 2, self.p.pair(axis))]

    def core_back(self, f):
        return [self.same(f, 9, 0, SHARDS, self.p.pair("c"))]

    def steps(self, path):
        seq = [(self.core, self.core_add)]
        for axis in path:
            if axis == "z":
                for k in range(1, LINE):
                    seq.append((functools.partial(self.z_copies, path=path, k=k, back=False), functools.partial(self.z_add, path=path, k=k)))
            else:
                seq.append((functools.partial(self.pair_send, path=path, axis=axis), functools.partial(self.pair_add, path=path, axis=axis)))
        for axis in path[::-1]:
            if axis == "z":
                for k in range(1, LINE):
                    seq.append((functools.partial(self.z_copies, path=path, k=k, back=True), None))
            else:
                seq.append((functools.partial(self.pair_back, path=path, axis=axis), None))
        seq.append((self.core_back, None))
        return seq

    def run_stage(self, f, s, path):
        seq = self.steps(path)
        if s > 0:
            copies, add = seq[s - 1]
            for cp in copies(f):
                if isinstance(cp, tuple):
                    sends, gets, one = cp
                    pl.when(sends)(one.wait_send)
                    pl.when(gets)(one.wait_recv)
                else:
                    cp.wait()
            if add is not None:
                add(f)
        if s < len(seq):
            for cp in seq[s][0](f):
                if isinstance(cp, tuple):
                    pl.when(cp[0])(cp[2].start)
                else:
                    cp.start()

    def stages(self, path):
        return len(self.steps(path)) + 1

    def step(self, i, last, paths, skew):
        n = self.stages(paths[0])
        for s in range(n - 1, -1, -1):
            f = i - s * skew

            def go(f=f, s=s):
                if s in (0, n - 1):
                    self.run_stage(f, s, paths[0])
                    return
                for core, path in enumerate(paths):
                    @pl.when(self.p.c == core)
                    def _():
                        self.run_stage(f, s, path)
            pl.when((f >= 0) & (f < last))(go)


PATHS = ("xzy", "yzx")
SKEW = 2
CHUNK = 256
SMALL = 16


def mm(a, b, ca=1, cb=0):
    return lax.dot_general(a, b, (((ca,), (cb,)), ((), ())), preferred_element_type=f32)


def gelu(v):
    return v * (0.5 * (1.0 + jnp.tanh(GELU_A * v * (1.0 + GELU_B * (v * v)))))


def gelu_both(v):
    sq = v * v
    t = jnp.tanh(GELU_A * v * (1.0 + GELU_B * sq))
    h = 0.5 * (1.0 + t)
    return v * h, h + 0.5 * v * (1.0 - t * t) * (GELU_A * (1.0 + 3.0 * GELU_B * sq))


def centred(v):
    c = v - jnp.mean(v, -1, keepdims=True)
    return c, lax.rsqrt(jnp.mean(c * c, -1, keepdims=True) + EPS)


def norm_back(c, rs, u):
    xh = c * rs
    return (u - jnp.mean(u, -1, keepdims=True) - xh * jnp.mean(u * xh, -1, keepdims=True)) * rs


def colsum(v):
    return jnp.sum(v, 0, keepdims=True)


def up16(n):
    return -(-n // 16) * 16


def up128(n):
    return -(-n // 128) * 128


class Sizes:
    def __init__(self, x_lo, x_hi, w_tok1_lo, w_chan_in):
        self.slots, self.q, self.d = x_lo.shape
        self.imgs = self.slots // 4
        self.qh = x_hi.shape[1]
        self.p, self.ph = 4 * self.q, 4 * self.qh
        self.ks = w_tok1_lo.shape[1]
        self.k = 4 * self.ks
        self.ff = w_chan_in.shape[1]
        self.chunks = self.ff // CHUNK
        self.pr = up16(self.p)
        self.own = 2 * self.qh
        self.hi0 = self.imgs * self.pr
        self.rows = self.hi0 + self.own
        self.wl, self.wh = up128(self.p), up128(self.ph)
        self.lanes = 2 * self.wl + 2 * self.wh + 256
        self.half_rows = CHUNK * (self.d // 256)
        self.t_lo = 3 * self.own
        self.t_rows = -(-(self.t_lo + self.k) // (16 * SHARDS)) * (16 * SHARDS)


def kernel(
    S,
    x_lo, x_hi, cot_lo, cot_hi, counts, wpack, bias_lo, bias_hi, w_in, w_out, b_in, b_out, gain1, shift1, gain2, shift2,
    out_lo, out_hi, grad_lo, grad_hi, g_sum, t_sum, s_sum,
    xl, xh, cl, ch, wg, bl, bh, w2t_lo, w1_lo, w2t_hi, w1_hi, bcol, af, nb, nh, n2, ct, tmp, gmh, hid, gp, winv, woutv,
    g, g_core, g_land, t, t_core, t_land, gw1, gw2, gb, sv, s1, s2,
    lo_send, lo_recv, hi_send, hi_recv, w_send, w_recv, ring_send, ring_recv, g_send, g_recv, t_send, t_recv,
    s_send, s_recv, local, g_kept, t_kept,
):
    p = Place()
    y, c = p.y, p.c
    m = y * 2 + c
    dpi = p.z * PAIR + p.x
    peers = [(y, 1 - c), (1 - y, c), (1 - y, 1 - c)]
    d = S.d

    def dev(yy, cc):
        return p.at(y=yy, c=cc)

    def rcopy(src, dst, send, recv, to):
        return pltpu.make_async_remote_copy(src, dst, send, recv, device_id=to, device_id_type=MESH)

    def dp_dev(k):
        i = (dpi + k) % (LINE * PAIR)
        return p.at(z=i // PAIR, x=i % PAIR)

    sem = pltpu.get_barrier_semaphore()
    for yy, cc in peers:
        pl.semaphore_signal(sem, inc=1, device_id=dev(yy, cc), device_id_type=MESH)
    for k in range(1, LINE * PAIR):
        pl.semaphore_signal(sem, inc=1, device_id=dp_dev(k), device_id_type=MESH)
    pl.semaphore_wait(sem, 3 + LINE * PAIR - 1)

    def lo_out(kind, i, src, dst):
        res = []
        for j, (yy, cc) in enumerate(peers):
            mm_ = yy * 2 + cc
            res.append(rcopy(src.at[S.imgs * mm_ + i], dst.at[m, i], lo_send.at[kind, j, i], lo_recv.at[kind, m, i], dev(yy, cc)))
        return res

    def lo_in(kind, i, dst):
        return [rcopy(dst.at[yy * 2 + cc, i], dst.at[yy * 2 + cc, i], lo_send.at[kind, j, i], lo_recv.at[kind, yy * 2 + cc, i], dev(yy, cc)) for j, (yy, cc) in enumerate(peers)]

    def lo_local(kind, i, src, dst):
        return pltpu.make_async_copy(src.at[S.imgs * m + i], dst.at[m, i], local.at[kind, i])

    def lo_back(kind, i, src, dst):
        return [rcopy(src.at[yy * 2 + cc, i], dst.at[S.imgs * m + i], lo_send.at[kind, j, i], lo_recv.at[kind, m, i], dev(yy, cc)) for j, (yy, cc) in enumerate(peers)]

    def lo_back_in(kind, i, dst):
        return [rcopy(dst.at[S.imgs * (yy * 2 + cc) + i], dst.at[S.imgs * (yy * 2 + cc) + i], lo_send.at[kind, j, i], lo_recv.at[kind, yy * 2 + cc, i], dev(yy, cc)) for j, (yy, cc) in enumerate(peers)]

    def lo_back_local(kind, i, src, dst):
        return pltpu.make_async_copy(src.at[m, i], dst.at[S.imgs * m + i], local.at[kind, i])

    def hi_out(kind, src, dst):
        res = []
        for h in range(2):
            mine = (y == h) & (c == y)
            ref = src.at[h] if src.shape[0] == 2 and len(src.shape) == 3 else src
            res.append((mine, rcopy(ref, dst.at[c], hi_send.at[kind, h], hi_recv.at[kind, c], dev(h, y)),
                        pltpu.make_async_copy(ref, dst.at[c], local.at[kind, S.imgs])))
        return res

    def hi_in(kind, dst):
        res = []
        for j in range(2):
            mine = (y == c) & (c == j)
            res.append((mine, rcopy(dst.at[j], dst.at[j], hi_send.at[kind, j], hi_recv.at[kind, j], dev(c, j))))
        return res

    def hi_back(kind, src, dst):
        res = []
        for j in range(2):
            mine = (y == c) & (c == j)
            res.append((mine, rcopy(src.at[j], dst.at[y], hi_send.at[kind, j], hi_recv.at[kind, y], dev(c, j)),
                        pltpu.make_async_copy(src.at[j], dst.at[y], local.at[kind, S.imgs])))
        return res

    def hi_back_in(kind, dst):
        res = []
        for h in range(2):
            mine = (y == h) & (c == y)
            res.append((mine, rcopy(dst.at[h], dst.at[h], hi_send.at[kind, h], hi_recv.at[kind, h], dev(h, y))))
        return res

    def start(copies):
        for cp in copies:
            cp.start()

    def start_hi(copies):
        for mine, remote, here in copies:
            pl.when(mine)(here.start)
            pl.when(jnp.logical_not(mine))(remote.start)

    def sent_hi(copies):
        for mine, remote, here in copies:
            pl.when(mine)(here.wait)
            pl.when(jnp.logical_not(mine))(remote.wait_send)

    def got_hi(copies):
        for mine, remote in copies:
            pl.when(jnp.logical_not(mine))(remote.wait_recv)

    my = (1 - y) * 2 + c
    w_own = pltpu.make_async_copy(wpack, wg.at[m], local.at[4, 0])
    w_y = rcopy(wpack, wg.at[m], w_send.at[0], w_recv.at[0], dev(1 - y, c))
    w_c = rcopy(wpack, wg.at[m], w_send.at[1], w_recv.at[1], dev(y, 1 - c))
    w_f = rcopy(wg.at[my], wg.at[my], w_send.at[2], w_recv.at[2], dev(y, 1 - c))
    w_own.start()
    w_y.start()
    w_c.start()
    start_hi(hi_out(0, x_hi, xh))
    bias_out = [rcopy(bias_lo, bl.at[m], w_send.at[3 + j], w_recv.at[3 + m], dev(yy, cc)) for j, (yy, cc) in enumerate(peers)]
    start(bias_out)
    bl[m] = bias_lo[...]
    bias_hi_out = hi_out(4, bias_hi, bh)
    start_hi(bias_hi_out)
    for i in range(S.imgs):
        start(lo_out(0, i, x_lo, xl))
        lo_local(0, i, x_lo, xl).start()
    start_hi(hi_out(1, cot_hi, ch))
    for i in range(S.imgs):
        start(lo_out(1, i, cot_lo, cl))
        lo_local(1, i, cot_lo, cl).start()
    load_in = pltpu.make_async_copy(w_in, winv, local.at[4, 1])
    load_out = pltpu.make_async_copy(w_out, woutv, local.at[4, 2])
    load_in.start()
    load_out.start()

    gv1, sv1 = gain1[...].astype(f32), shift1[...].astype(f32)
    gv2, sv2 = gain2[...].astype(f32), shift2[...].astype(f32)
    hi = pl.ds(S.hi0, S.own)
    own = pl.ds(pl.multiple_of(c * S.own, 16), S.own)

    def img(i):
        return pl.ds(pl.multiple_of(i * S.pr, 16), S.pr)

    def gather_rows(block, i):
        for s in range(4):
            tmp[s * S.q:(s + 1) * S.q, :] = block[s, i].astype(f32)
        if S.pr > S.p:
            tmp[S.p:S.pr, :] = jnp.zeros((S.pr - S.p, d), f32)

    def scatter_rows(block, i):
        for s in range(4):
            block[s, i] = tmp[s * S.q:(s + 1) * S.q, :].astype(bf16)

    sv[...] = jnp.zeros_like(sv)
    t[...] = jnp.zeros_like(t)
    gw1[...] = jnp.zeros_like(gw1)
    gw2[...] = jnp.zeros_like(gw2)

    got_hi(hi_in(0, xh))
    sent_hi(hi_out(0, x_hi, xh))
    v = xh[...].reshape(S.own, d).astype(f32)
    cen, rs = centred(v)
    n = (cen * rs * gv1 + sv1).astype(bf16)
    nb[hi, :] = n
    nh[own, :] = n
    af[hi, :] = v
    nh_copy = rcopy(nh.at[own], nh.at[own], ring_send.at[0], ring_recv.at[0], dev(y, 1 - c))
    nh_copy.start()

    w_own.wait()
    w_y.wait()
    w_f.start()
    w_c.wait()
    w_f.wait()
    o1, o2, o3, o4 = S.wl, 2 * S.wl, 2 * S.wl + S.wh, 2 * S.wl + 2 * S.wh

    def w1t_lo():
        return wg[:, :, 0:S.pr].reshape(S.k, S.pr)

    def w2_lo():
        return wg[:, :, o1:o1 + S.pr].reshape(S.k, S.pr)

    def w1t_hi():
        return wg[:, :, o2:o2 + S.ph].reshape(S.k, S.ph)

    def w2_hi():
        return wg[:, :, o3:o3 + S.ph].reshape(S.k, S.ph)

    def b1_lo():
        return wg[:, :, o4:o4 + 128].reshape(S.k, 128).astype(f32)[:, 0:1]

    def b1_hi():
        return wg[:, :, o4 + 128:o4 + 256].reshape(S.k, 128).astype(f32)[:, 0:1]

    w1_lo[...] = w1t_lo().T
    w2t_lo[...] = w2_lo().T
    w1_hi[...] = w1t_hi().T
    w2t_hi[...] = w2_hi().T
    for j, (yy, cc) in enumerate(peers):
        bias_out[j].wait_send()
        s = yy * 2 + cc
        rcopy(bl.at[s], bl.at[s], w_send.at[3 + j], w_recv.at[3 + s], dev(yy, cc)).wait_recv()
    got_hi(hi_in(4, bh))
    sent_hi(bias_hi_out)
    bcol[...] = jnp.zeros_like(bcol)
    for s in range(4):
        bcol[s * S.q:(s + 1) * S.q, :] = bl[s].astype(f32)

    def fwd_lo(i, carry):
        for cp in lo_in(0, i, xl):
            cp.wait_recv()
        lo_local(0, i, x_lo, xl).wait()
        gather_rows(xl, i)
        v = tmp[...]
        cen, rs = centred(v)
        n = (cen * rs * gv1 + sv1).astype(bf16)
        nb[img(i), :] = n
        ht = gelu(mm(w1t_lo(), n) + b1_lo()).astype(bf16)
        af[img(i), :] = v + (mm(w2t_lo[...], ht) + bcol[:, 0:1])
        return carry

    lax.fori_loop(0, S.imgs, fwd_lo, 0)
    nh_copy.wait()
    ht = gelu(mm(w1t_hi(), nh[...]) + b1_hi()).astype(bf16)
    bcol_hi = bh[...].reshape(S.own, 128).astype(f32)[:, 0:1]
    af[hi, :] = af[hi, :] + (mm(w2t_hi[own, :], ht) + bcol_hi)

    def norm_two(rows):
        cen, rs = centred(af[rows, :])
        n2[rows, :] = (cen * rs * gv2 + sv2).astype(bf16)

    norm_two(hi)

    def norm_lo(i, carry):
        norm_two(img(i))
        return carry

    lax.fori_loop(0, S.imgs, norm_lo, 0)

    def live_lo(i):
        return jnp.where(S.imgs * m + i < counts[0, 0], 1.0, 0.0).astype(f32)

    live_hi = jnp.where(y < counts[0, 1], 1.0, 0.0).astype(f32)
    got_hi(hi_in(1, ch))
    sent_hi(hi_out(1, cot_hi, ch))
    ct[hi, :] = (ch[...].reshape(S.own, d).astype(f32) * live_hi).astype(bf16)

    def cot_rows(i, carry):
        for cp in lo_in(1, i, cl):
            cp.wait_recv()
        lo_local(1, i, cot_lo, cl).wait()
        gather_rows(cl, i)
        ct[img(i), :] = (tmp[...] * live_lo(i)).astype(bf16)
        return carry

    lax.fori_loop(0, S.imgs, cot_rows, 0)
    for kind, src, dst in ((0, x_lo, xl), (1, cot_lo, cl)):
        for i in range(S.imgs):
            for cp in lo_out(kind, i, src, dst):
                cp.wait_send()
    load_in.wait()
    load_out.wait()

    def channel(f):
        cols = pl.ds(pl.multiple_of(f * CHUNK, CHUNK), CHUNK)
        h, slope = gelu_both(mm(n2[...], winv[:, cols]) + b_in[:, cols].astype(f32))
        hb = h.astype(bf16)
        hid[:, cols] = hb
        gpre = (mm(ct[...], woutv[cols, :], 1, 1) * slope).astype(bf16)
        gp[:, cols] = gpre
        gb[:, cols] = colsum(gpre.astype(f32))
        g[f, 0:d, :] = mm(n2[...], gpre, 0, 0).astype(bf16)
        grad = mm(hb, ct[...], 0, 0)
        for j in range(d // 256):
            g[f, S.half_rows + CHUNK * j:S.half_rows + CHUNK * (j + 1), :] = grad[:, 256 * j:256 * (j + 1)].astype(bf16)

    bo = b_out[...].astype(f32)

    def channel_back(rows, live):
        a = af[rows, :]
        out = (a + mm(hid[rows, :], woutv[...]) + bo) * live
        gn = mm(gp[rows, :], winv[...], 1, 1)
        cen, rs = centred(a)
        c_rows = ct[rows, :].astype(f32)
        grad = c_rows + norm_back(cen, rs, gn * gv2)
        sv[0:1, :] += colsum(c_rows)
        sv[1:2, :] += colsum(gn * (cen * rs))
        sv[2:3, :] += colsum(gn)
        af[rows, :] = grad
        n2[rows, :] = grad.astype(bf16)
        return out

    def back_hi():
        out = channel_back(hi, live_hi)
        ch[...] = out.astype(bf16).reshape(2, S.qh, d)
        start_hi(hi_back(2, ch, out_hi))
        gmh[own, :] = n2[hi, :]
        gm_copy.start()

    gm_copy = rcopy(gmh.at[own], gmh.at[own], ring_send.at[1], ring_recv.at[1], dev(y, 1 - c))

    def back_lo(i):
        tmp[...] = channel_back(img(i), live_lo(i))
        scatter_rows(cl, i)
        start(lo_back(2, i, cl, out_lo))
        lo_back_local(2, i, cl, out_lo).start()

    ones = jnp.ones((8, d), bf16)

    def first_norm_back(v, gn, rows):
        cen, rs = centred(v)
        sv[3:4, :] += colsum(gn * (cen * rs))
        sv[4:5, :] += colsum(gn)
        return af[rows, :] + norm_back(cen, rs, gn * gv1)

    def token_lo(i):
        n = nb[img(i), :]
        gm = n2[img(i), :]
        h, slope = gelu_both(mm(w1t_lo(), n) + b1_lo())
        gw2[:, 0:S.pr] += mm(h.astype(bf16), gm, 1, 1)
        gpt = (mm(w2_lo(), gm) * slope).astype(bf16)
        gw1[:, 0:S.pr] += mm(gpt, n, 1, 1)
        sv[9:10, 0:S.k] += mm(ones, gpt, 1, 1)[0:1]
        sv[10:11, 0:S.pr] += mm(ones, gm, 1, 1)[0:1]
        gn = mm(w1_lo[...], gpt)
        gather_rows(xl, i)
        tmp[...] = first_norm_back(tmp[...], gn, img(i))
        scatter_rows(xl, i)
        start(lo_back(3, i, xl, grad_lo))
        lo_back_local(3, i, xl, grad_lo).start()

    def token_hi():
        gm_copy.wait()
        n = nb[hi, :]
        gm = n2[hi, :]
        h, slope = gelu_both(mm(w1t_hi(), nh[...]) + b1_hi())
        ga2 = mm(gm, h.astype(bf16), 1, 1)
        gpt = (mm(w2_hi(), gmh[...]) * slope).astype(bf16)
        ga1 = mm(n, gpt, 1, 1)
        once = jnp.where(c == 0, 1.0, 0.0).astype(f32)
        sv[11:12, 0:S.k] += mm(ones, gpt, 1, 1)[0:1] * once
        sv[pl.ds(12 + c, 1), 0:S.own] = mm(ones, gm, 1, 1)[0:1]
        gn = mm(w1_hi[own, :], gpt)
        grad = first_norm_back(xh[...].reshape(S.own, d).astype(f32), gn, hi)
        xh[...] = grad.astype(bf16).reshape(2, S.qh, d)
        start_hi(hi_back(3, xh, grad_hi))
        for j in range(S.ff // d):
            sv[5 + j:6 + j, :] = gb[:, d * j:d * (j + 1)]
        for k in range(2):
            @pl.when(c == k)
            def _():
                t[0, S.t_rows * k:S.t_rows * k + S.own, :] = ga1[:, 0:256].astype(bf16)
                t[0, S.t_rows * k + S.own:S.t_rows * k + 2 * S.own, :] = ga2[:, 0:256].astype(bf16)
                t[0, S.t_rows * k + 2 * S.own:S.t_rows * k + 3 * S.own, 0:128] = ga1[:, 256:384].astype(bf16)
                t[0, S.t_rows * k + 2 * S.own:S.t_rows * k + 3 * S.own, 128:256] = ga2[:, 256:384].astype(bf16)
        t[0, S.t_lo:S.t_lo + S.k, :] = gw1[...].astype(bf16)
        t[0, S.t_rows + S.t_lo:S.t_rows + S.t_lo + S.k, :] = gw2[...].astype(bf16)
        s1[m] = sv[...]
        start(s1_out)

    s1_out = [rcopy(s1.at[m], s1.at[m], s_send.at[j], s_recv.at[m], dev(yy, cc)) for j, (yy, cc) in enumerate(peers)]
    s2_out = [rcopy(s2.at[dpi], s2.at[dpi], s_send.at[3 + k], s_recv.at[4 + dpi], dp_dev(k)) for k in range(1, LINE * PAIR)]

    ar = AllReduce(p, g, g_core, g_land, g_sum, g_send, g_recv, g_kept)
    art = AllReduce(p, t, t_core, t_land, t_sum, t_send, t_recv, t_kept)
    stages = ar.stages(PATHS[0])
    nc = S.chunks
    b0 = nc + 1 + S.imgs
    t0 = b0 + S.imgs

    def step(i, carry):
        pl.when(i < nc)(lambda: channel(i))
        pl.when(i == nc)(back_hi)
        pl.when((i > nc) & (i < b0))(lambda: back_lo(i - nc - 1))
        pl.when((i >= b0) & (i < t0))(lambda: token_lo(i - b0))
        pl.when(i == t0)(token_hi)
        ar.step(i, nc, PATHS, SKEW)
        art.step(i - t0, 1, PATHS, 1)
        return carry

    lax.fori_loop(0, max(nc + (stages - 1) * SKEW, t0 + stages), step, 0)

    for j, (yy, cc) in enumerate(peers):
        s = yy * 2 + cc
        s1_out[j].wait_send()
        rcopy(s1.at[s], s1.at[s], s_send.at[j], s_recv.at[s], dev(yy, cc)).wait_recv()
    s2[dpi] = s1[0] + s1[1] + s1[2] + s1[3]
    start(s2_out)
    for k in range(1, LINE * PAIR):
        i = (dpi + k) % (LINE * PAIR)
        s2_out[k - 1].wait_send()
        rcopy(s2.at[i], s2.at[i], s_send.at[3 + k], s_recv.at[4 + i], dp_dev(k)).wait_recv()
    total = s2[0]
    for i in range(1, LINE * PAIR):
        total = total + s2[i]
    s_sum[...] = total

    for kind, src, src_hi, dst, dst_hi in ((2, cl, ch, out_lo, out_hi), (3, xl, xh, grad_lo, grad_hi)):
        for i in range(S.imgs):
            for cp in lo_back(kind, i, src, dst):
                cp.wait_send()
            for cp in lo_back_in(kind, i, dst):
                cp.wait_recv()
            lo_back_local(kind, i, src, dst).wait()
        sent_hi(hi_back(kind, src_hi, dst_hi))
        got_hi(hi_back_in(kind, dst_hi))


def mixer(S, args):
    V = pl.BlockSpec(memory_space=pltpu.VMEM)
    A = pl.BlockSpec(memory_space=pl.ANY)
    M = pl.BlockSpec(memory_space=pltpu.SMEM)
    sds = jax.ShapeDtypeStruct
    d, dma = S.d, pltpu.SemaphoreType.DMA
    nc = S.chunks
    unit = 2 * S.half_rows // (2 * SHARDS)
    tu = S.t_rows // SHARDS
    scratch = [
        pltpu.VMEM((4, S.imgs, S.q, d), bf16), pltpu.VMEM((2, S.qh, d), bf16),
        pltpu.VMEM((4, S.imgs, S.q, d), bf16), pltpu.VMEM((2, S.qh, d), bf16),
        pltpu.VMEM((4, S.ks, S.lanes), bf16), pltpu.VMEM((4, S.q, 128), bf16), pltpu.VMEM((2, S.qh, 128), bf16),
        pltpu.VMEM((S.pr, S.k), bf16), pltpu.VMEM((S.pr, S.k), bf16), pltpu.VMEM((S.ph, S.k), bf16), pltpu.VMEM((S.ph, S.k), bf16),
        pltpu.VMEM((S.pr, 128), f32),
        pltpu.VMEM((S.rows, d), f32), pltpu.VMEM((S.rows, d), bf16), pltpu.VMEM((S.ph, d), bf16), pltpu.VMEM((S.rows, d), bf16),
        pltpu.VMEM((S.rows, d), bf16), pltpu.VMEM((S.pr, d), f32), pltpu.VMEM((S.ph, d), bf16),
        pltpu.VMEM((S.rows, S.ff), bf16), pltpu.VMEM((S.rows, S.ff), bf16), pltpu.VMEM((d, S.ff), bf16), pltpu.VMEM((S.ff, d), bf16),
        pltpu.VMEM((nc, 2 * SHARDS * unit, 256), bf16), pltpu.VMEM((2 * SKEW, SHARDS * unit, 256), bf16), pltpu.VMEM((nc, LANDED * unit, 256), bf16),
        pltpu.VMEM((1, 2 * S.t_rows, 256), bf16), pltpu.VMEM((1, S.t_rows, 256), bf16), pltpu.VMEM((1, LANDED * tu, 256), bf16),
        pltpu.VMEM((S.k, 256), f32), pltpu.VMEM((S.k, 256), f32), pltpu.VMEM((1, S.ff), f32),
        pltpu.VMEM((SMALL, d), f32), pltpu.VMEM((4, SMALL, d), f32), pltpu.VMEM((LINE * PAIR, SMALL, d), f32),
        dma((4, 3, S.imgs)), dma((4, 4, S.imgs)), dma((5, 2)), dma((5, 2)), dma((6,)), dma((7,)), dma((2,)), dma((2,)),
        dma((nc, NSEM)), dma((nc, NSEM)), dma((1, NSEM)), dma((1, NSEM)), dma((11,)), dma((12,)), dma((5, S.imgs + 1)), dma((nc,)), dma((1,)),
    ]
    return pl.pallas_call(
        functools.partial(kernel, S),
        out_shape=(
            sds((S.slots, S.q, d), bf16), sds((2, S.qh, d), bf16), sds((S.slots, S.q, d), bf16), sds((2, S.qh, d), bf16),
            sds((nc, 2 * S.half_rows, 256), bf16), sds((1, 2 * S.t_rows, 256), bf16), sds((SMALL, d), f32),
        ),
        in_specs=[A, A, A, A, M, A, V, V, A, A, V, V, V, V, V, V],
        out_specs=(A, A, A, A, A, A, V),
        scratch_shapes=scratch,
        compiler_params=pltpu.CompilerParams(collective_id=0, has_side_effects=True, vmem_limit_bytes=63 * 1024 * 1024),
    )(*args)


def widen(S, g):
    d = S.d

    def place(g_ref, in_ref, out_ref):
        in_ref[...] = g_ref[0, 0:d, :].astype(f32)
        for j in range(d // 256):
            out_ref[:, 256 * j:256 * (j + 1)] = g_ref[0, S.half_rows + CHUNK * j:S.half_rows + CHUNK * (j + 1), :].astype(f32)

    return pl.pallas_call(
        place,
        grid=(S.chunks,),
        out_shape=(jax.ShapeDtypeStruct((d, S.ff), f32), jax.ShapeDtypeStruct((S.ff, d), f32)),
        in_specs=[pl.BlockSpec((1, 2 * S.half_rows, 256), lambda i: (i, 0, 0))],
        out_specs=(pl.BlockSpec((d, CHUNK), lambda i: (0, i)), pl.BlockSpec((CHUNK, d), lambda i: (i, 0))),
    )(g)


def body(
    groups,
    x_lo, x_hi, cot_lo, cot_hi, counts, ln1_gain, ln1_bias, w_tok1_lo, b_tok1_lo, w_tok2_lo, b_tok2_lo, w_tok1_hi, b_tok1_hi,
    w_tok2_hi, b_tok2_hi, ln2_gain, ln2_bias, w_chan_in, b_chan_in, w_chan_out, b_chan_out,
):
    S = Sizes(x_lo, x_hi, w_tok1_lo, w_chan_in)

    def lanes(w, n):
        return jnp.pad(w, ((0, 0), (0, n - w.shape[1])))

    def column(b):
        return jnp.broadcast_to(b[:, None], (b.shape[0], 128))

    wpack = jnp.concatenate(
        [lanes(w_tok1_lo.T, S.wl), lanes(w_tok2_lo, S.wl), lanes(w_tok1_hi.T, S.wh), lanes(w_tok2_hi, S.wh), column(b_tok1_lo), column(b_tok1_hi)],
        axis=1,
    )
    row = lambda v: v[None, :]
    out_lo, out_hi, grad_lo, grad_hi, g, t, s = mixer(
        S,
        (x_lo, x_hi, cot_lo, cot_hi, counts, wpack, column(b_tok2_lo), column(b_tok2_hi), w_chan_in, w_chan_out, row(b_chan_in), row(b_chan_out),
         row(ln1_gain), row(ln1_bias), row(ln2_gain), row(ln2_bias)),
    )
    g_in, g_out = widen(S, g)
    t = t.astype(f32).reshape(2, S.t_rows, 256)
    if groups is not None:
        g_in, g_out, t, s = lax.psum((g_in, g_out, t, s), "dp", axis_index_groups=groups)
    m = lax.axis_index("mp")
    ks = m * S.ks
    lo1 = lax.dynamic_slice(t[0], (S.t_lo + ks, 0), (S.ks, 256))[:, :S.p].T
    lo2 = lax.dynamic_slice(t[1], (S.t_lo + ks, 0), (S.ks, 256))[:, :S.p]
    n = S.own
    hi1 = jnp.concatenate([t[:, 0:n], t[:, 2 * n:3 * n, 0:128]], axis=2).reshape(2 * n, 384)
    hi2 = jnp.concatenate([t[:, n:2 * n], t[:, 2 * n:3 * n, 128:256]], axis=2).reshape(2 * n, 384)
    hi1 = lax.dynamic_slice(hi1, (0, ks), (S.ph, S.ks))
    hi2 = lax.dynamic_slice(hi2, (0, ks), (S.ph, S.ks)).T
    b2_hi = jnp.concatenate([s[12, :n], s[13, :n]])
    cut = lambda v, w: lax.dynamic_slice(v, (m * w,), (w,))
    return (
        out_lo, out_hi, grad_lo.astype(f32), grad_hi.astype(f32), s[3], s[4],
        lo1, cut(s[9], S.ks), lo2, cut(s[10], S.q), hi1, cut(s[11], S.ks), hi2, cut(b2_hi, S.qh),
        s[1], s[2], g_in, s[5:9].reshape(S.ff), g_out, s[0],
    )


def solution(mesh):
    blocks = mesh.shape["dp"] // (LINE * PAIR)
    groups = None
    if blocks > 1:
        size = LINE * PAIR
        groups = [[b * size + i for b in range(blocks)] for i in range(size)]
    tokens, rows = P("dp", "mp", None), P("dp", None)
    col, row, vec, rep = P(None, "mp"), P("mp", None), P("mp"), P()
    return jax.shard_map(
        functools.partial(body, groups),
        mesh=mesh,
        in_specs=(tokens,) * 4 + (rows, rep, rep) + (col, vec, row, vec) * 2 + (rep,) * 6,
        out_specs=(tokens,) * 4 + (rep, rep) + (col, vec, row, vec) * 2 + (rep,) * 6,
        check_vma=False,
    )
```

time: 1000 us -> 241 us (0.24)
  waiting for transfers between devices: 702 us -> 0 us
  Pallas kernels: 0 us -> 211 us
  matrix products: 109 us -> 0 us
  blocking collectives: 62.5 us -> 0 us
  local copies, waits for them, and re-layouts: 65.8 us -> 23.7 us
  other arithmetic: 40.9 us -> 4.14 us
  between operations: 15.7 us -> 0.79 us
    psum x2 -> x0, waiting for transfers between devices: 339 us -> none  [the longest x1 311 us: body(): lax.psum((grad_gain_one, grad_shift_one, grad_gain_two, grad_shift_two, g...]
    pallas_call x0 -> x2, Pallas kernels: none -> 211 us  [the longest x1 199 us: mixer(): pl.pallas_call(functools.partial(kernel, S), out_shape=(sds((S.slots, S.q...]
    unnamed x12 -> x0, waiting for transfers between devices: 192 us -> none
    dot_general x18 -> x0, matrix products: 109 us -> none  [the longest x1 16.1 us: channel_backward(): jnp.einsum('rd,fd->rf', grad_bf, w_chan_out, preferred_element_type=jnp.f...]
    all_gather x4 -> x0, waiting for transfers between devices: 96.5 us -> none  [the longest x1 38.8 us: body(): lax.all_gather(normed_lo, 'mp', axis=1, tiled=True)]
    reduce_scatter x2 -> x0, waiting for transfers between devices: 74.8 us -> none  [the longest x1 37.4 us: body(): lax.psum_scatter(back_hi[0], 'mp', scatter_dimension=1, tiled=True)]
    psum x2 -> x0, blocking collectives: 62.5 us -> none  [the longest x1 40.6 us: body(): lax.psum((grad_gain_one, grad_shift_one, grad_gain_two, grad_shift_two, g...]
    unnamed x137 -> x23, local copies, waits for them, and re-layouts: 31.9 us -> 7.67 us
  transfers between devices with their start and end apart: 10 -> 0, of which waited for: 10 -> 0; matrix products, arithmetic and copies ran while one was open for 11% -> 0% of each run, Pallas kernels for 0% -> 0%
where the time goes in v1:
time: 241 us; the launch traced here: 240 us
  Pallas kernels  211 us (88%)
  local copies, waits for them, and re-layouts  23.7 us (10%)
  other arithmetic  4.14 us (2%)
    pallas_call x1, Pallas kernels, mixer(): pl.pallas_call(functools.partial(kernel, S), out_shape=(sds((S.slots, S.q...  199 us
    pallas_call x1, Pallas kernels, widen(): pl.pallas_call(place, grid=(S.chunks,), out_shape=(jax.ShapeDtypeStruct((...  12.6 us
    unnamed x23, local copies, waits for them, and re-layouts  7.67 us
    broadcast_in_dim x6, local copies, waits for them, and re-layouts, body(): row = lambda v: v[None, :]  7.61 us

profile of v1, /device:TPU:0, one launch (start us, length us, event | category | flops | bytes accessed | tf_op | source)
XLA Modules:
  0.0 239.8 jit_solution(6272450218833740293)
XLA Ops:
  0.7 0.8 pad_dynamic-update-slice_fusion.3
  1.5 0.8 pad_dynamic-update-slice_fusion.2
  2.3 0.9 pad_dynamic-update-slice_fusion.1
  3.2 0.9 pad_dynamic-update-slice_fusion
  4.1 0.7 constant_dynamic-update-slice_fusion.1
  4.9 0.7 constant_dynamic-update-slice_fusion.wpack
  5.6 1.4 broadcast_in_dim.45.bias_hi
  7.0 1.3 broadcast_in_dim.44.bias_lo
  8.4 1.3 broadcast_in_dim.46.b_in
  9.7 1.3 broadcast_in_dim.47.b_out
  10.9 1.3 broadcast_in_dim.48.gain1
  12.2 1.3 broadcast_in_dim.49.shift1
  13.4 1.3 broadcast_in_dim.50.gain2
  14.7 1.3 broadcast_in_dim.51.shift2
  16.0 198.6 %shard_map.356 = (bf16[12,49,768]{2,1,0:T(8,128)(2,1)}, bf16[2,144,768]{2,1,0:T(8,128)(2,1)}, bf16[12,49,768]{2,1,0:T(8,128)(2,1)}, bf16[2,144,768]{2,1,0:T(8,12...) custom-call(bf16[12,49,768]{2,1,0:T(8,128)(2,1)} %x_lo.1, ...), custom_call_target="tpu_custom_call" | custom-call | tf_op jit(solution)/shard_map/pallas_call | solution.py:699
  214.6 1.5 convert_element_type.17
  216.5 0.9 copy.44
  217.5 0.9 copy.43
  219.8 0.7 dynamic-slice_bitcast_fusion.1
  223.1 12.6 %shard_map.357 = (f32[768,3072]{1,0:T(8,128)}, f32[3072,768]{1,0:T(8,128)}) custom-call(bf16[12,1536,256]{2,1,0:T(8,128)(2,1)} %get-tuple-element.35.g_ref), custom_call_target="tpu_custom_call" | custom-call | tf_op jit(solution)/shard_map/pallas_call | solution.py:720
  235.7 1.5 convert_element_type.15
  237.1 1.0 convert_element_type.16
  238.1 1.0 copy.52
  239.1 0.8 copy.53
  (29 shorter events, 4.6 us)
Async XLA Ops:
  5.6 10.3 %copy-start.3 = (bf16[96,2048]{1,0:T(8,128)(2,1)}, bf16[96,2048]{1,0:T(8,128)(2,1)S(1)}, u32[]{:S(2)}) copy-start(bf16[96,2048]{1,0:T(8,128)(2,1)S(1)} %constant_dynamic-update-slice_fusion.wpack) | copy-start | bytes 1179652
  216.2 2.2 copy-start.6
  216.4 3.3 %copy-start = (bf16[1,2560,256]{2,1,0:T(8,128)(2,1)S(1)}, bf16[1,2560,256]{2,1,0:T(8,128)(2,1)}, u32[]{:S(2)}) copy-start(bf16[1,2560,256]{2,1,0:T(8,128)(2,1)} %get-tuple-element.34) | copy-start | bytes 3932164
  223.1 12.6 %copy-start.1 = (bf16[12,49,768]{2,1,0:T(8,128)(2,1)S(1)}, bf16[12,49,768]{2,1,0:T(8,128)(2,1)}, u32[]{:S(2)}) copy-start(bf16[12,49,768]{2,1,0:T(8,128)(2,1)} %get-tuple-element.31) | copy-start | bytes 2709508
  235.7 1.5 copy-start.5
  235.7 2.4 %copy-start.2 = (bf16[12,49,768]{2,1,0:T(8,128)(2,1)S(1)}, bf16[12,49,768]{2,1,0:T(8,128)(2,1)}, u32[]{:S(2)}) copy-start(bf16[12,49,768]{2,1,0:T(8,128)(2,1)} %get-tuple-element.105) | copy-start | bytes 2709508
  237.1 1.9 copy-start.4

commit v2 on v1

--- a/solution.py
+++ b/solution.py
@@ -14,10 +14,9 @@
 
 LINE, PAIR = 4, 2
 SHARDS = 16
-LAND = {"xzy": dict(x=(0, 8), z=(8, 10), y=(18, 1)),
-        "yzx": dict(y=(0, 8), z=(8, 10), x=(18, 1))}
+LAND = {"xzy": dict(x=0, z=8, y=18), "yzx": dict(y=0, z=8, x=18)}
 LANDED = 19
-NSEM = 10
+CORE, X, Y, UP, DOWN, X_BACK, Y_BACK, UP_BACK, DOWN_BACK, CORE_BACK, NSEM = 0, 1, 2, 2, 5, 9, 10, 10, 13, 17, 18
 
 
 class Place:
@@ -66,146 +65,141 @@
     def copy(self, f, k, src, dst, dev):
         return pltpu.make_async_remote_copy(src, dst, self.send.at[f, k], self.recv.at[f, k], device_id=dev, device_id_type=MESH)
 
+    def rows(self, start, n):
+        return self.sh(self.p.c * SHARDS + start, n)
+
     def half(self, f, start, n):
-        return self.g.at[f, self.sh(self.p.c * SHARDS + start, n)]
+        return self.g.at[f, self.rows(start, n)]
+
+    def done(self, f, start, n):
+        return self.out.at[f, self.rows(start, n)]
+
+    def land(self, f, start, n):
+        return self.l.at[f, self.sh(start, n)]
+
+    def added(self, f, start, n, off):
+        return lambda: add_into(self.g, (f, self.rows(start, n)), self.l[f, self.sh(off, n)])
 
     def core(self, f):
         p = self.p
-        return [self.copy(f, 0, self.g.at[f, self.sh((1 - p.c) * SHARDS, SHARDS)], self.lc.at[f % self.lc.shape[0]], p.pair("c"))]
-
-    def core_add(self, f):
-        add_into(self.g, (f, self.sh(self.p.c * SHARDS, SHARDS)), self.lc[f % self.lc.shape[0]])
+        slot = f % self.lc.shape[0]
+        src = self.g.at[f, self.sh((1 - p.c) * SHARDS, SHARDS)]
+        return [(None, None, self.copy(f, CORE, src, self.lc.at[slot], p.pair("c")),
+                 lambda: add_into(self.g, (f, self.rows(0, SHARDS)), self.lc[slot]))]
 
     def regions(self, path):
         base, n, out = 0, SHARDS, {}
         for axis in path:
             out[axis] = (base, n)
-            parts = LINE if axis == "z" else PAIR
-            n = n // parts
+            n = n // (LINE if axis == "z" else PAIR)
             base = base + getattr(self.p, axis) * n
         out["end"] = (base, n)
         return out
 
-    def pair_send(self, f, path, axis):
+    def pair(self, f, path, axis):
         base, n = self.regions(path)[axis]
-        other = 1 - getattr(self.p, axis)
-        off, m = LAND[path][axis]
-        k = {"x": 1, "y": 2}[axis]
-        return [self.copy(f, k, self.half(f, base + other * (n // 2), n // 2), self.l.at[f, self.sh(off, m)], self.p.pair(axis))]
-
-    def pair_add(self, f, path, axis):
-        base, n = self.regions(path)[axis]
-        off, m = LAND[path][axis]
-        s = self.p.c * SHARDS + base + getattr(self.p, axis) * m
-        add_into(self.g, (f, self.sh(s, m)), self.l[f, self.sh(off, m)])
-
-    def z_copies(self, f, path, k, back):
+        mine, off, m = getattr(self.p, axis), LAND[path][axis], n // 2
+        k = {"x": X, "y": Y}[axis]
+        return [(None, None, self.copy(f, k, self.half(f, base + (1 - mine) * m, m), self.land(f, off, m), self.p.pair(axis)),
+                 self.added(f, base + mine * m, m, off))]
+
+    def line(self, f, path, k):
         base, n = self.regions(path)["z"]
-        m = n // LINE
-        off, _ = LAND[path]["z"]
-        z = self.p.z
-        if back:
-            up, down = self.done(f, base, k * m), self.done(f, base + (LINE - k) * m, k * m)
-            up = self.copy(f, 7, up, up, self.p.up())
-            down = self.copy(f, 8, down, down, self.p.down())
-        else:
-            w = (LINE - k) * m
-            up = self.copy(f, 3, self.half(f, base + k * m, w), self.l.at[f, self.sh(off, w)], self.p.up())
-            down = self.copy(f, 4, self.half(f, base, w), self.l.at[f, self.sh(off + (k + 1) * m, w)], self.p.down())
-        return [(z == k - 1, z == k, up), (z == LINE - k, z == LINE - 1 - k, down)]
-
-    def z_add(self, f, path, k):
-        base, n = self.regions(path)["z"]
-        m = n // LINE
-        off, _ = LAND[path]["z"]
-        c0 = self.p.c * SHARDS + base
-        w = (LINE - k) * m
-
-        @pl.when(self.p.z == k)
-        def _():
-            add_into(self.g, (f, self.sh(c0 + k * m, w)), self.l[f, self.sh(off, w)])
-
-        @pl.when(self.p.z == LINE - 1 - k)
-        def _():
-            add_into(self.g, (f, self.sh(c0, w)), self.l[f, self.sh(off + (k + 1) * m, w)])
-
-    def done(self, f, start, n):
-        return self.out.at[f, self.sh(self.p.c * SHARDS + start, n)]
-
-    def same(self, f, k, start, n, dev):
-        ref = self.done(f, start, n)
-        return self.copy(f, k, ref, ref, dev)
+        z, m = self.p.z, n // LINE
+        off = LAND[path]["z"]
+        above, below = off + (LINE - 1 - k) * m, off + (1 + k) * m
+        inside = lambda p: base + jnp.clip(p, 0, LINE - 1) * m
+        up = self.copy(f, UP + k, self.half(f, inside(z + LINE - k), m), self.land(f, above, m), self.p.up())
+        down = self.copy(f, DOWN + k, self.half(f, inside(z - LINE + k), m), self.land(f, below, m), self.p.down())
+        return [((z < LINE - 1) & (z <= k - 1), (z > 0) & (z <= k), up, self.added(f, inside(z + LINE - 1 - k), m, above)),
+                ((z > 0) & (z >= LINE - k), (z < LINE - 1) & (z >= LINE - 1 - k), down, self.added(f, inside(z - LINE + 1 + k), m, below))]
 
     def pair_back(self, f, path, axis):
         base, n = self.regions(path)[axis]
-        k = {"x": 5, "y": 6}[axis]
+        at, m = base + getattr(self.p, axis) * (n // 2), n // 2
+        k = {"x": X_BACK, "y": Y_BACK}[axis]
+        ref = self.done(f, at, m)
         if axis == path[-1]:
-            at, ref = self.regions(path)["end"]
-            src, dst = self.half(f, at, ref), self.done(f, at, ref)
-            return [self.copy(f, k, src, dst, self.p.pair(axis)), pltpu.make_async_copy(src, dst, self.kept.at[f])]
-        return [self.same(f, k, base + getattr(self.p, axis) * (n // 2), n // 2, self.p.pair(axis))]
+            src = self.half(f, at, m)
+            return [(None, None, self.copy(f, k, src, ref, self.p.pair(axis)), None),
+                    (None, None, pltpu.make_async_copy(src, ref, self.kept.at[f]), None)]
+        return [(None, None, self.copy(f, k, ref, ref, self.p.pair(axis)), None)]
+
+    def line_back(self, f, path, k):
+        base, n = self.regions(path)["z"]
+        z, m = self.p.z, n // LINE
+        inside = lambda p: self.done(f, base + jnp.clip(p, 0, LINE - 1) * m, m)
+        up, down = inside(z + 1 - k), inside(z + k - 1)
+        return [((z < LINE - 1) & (z >= k - 1), (z > 0) & (z >= k), self.copy(f, UP_BACK + k, up, up, self.p.up()), None),
+                ((z > 0) & (z <= LINE - k), (z < LINE - 1) & (z <= LINE - 1 - k), self.copy(f, DOWN_BACK + k, down, down, self.p.down()), None)]
 
     def core_back(self, f):
-        return [self.same(f, 9, 0, SHARDS, self.p.pair("c"))]
+        ref = self.done(f, 0, SHARDS)
+        return [(None, None, self.copy(f, CORE_BACK, ref, ref, self.p.pair("c")), None)]
 
     def steps(self, path):
-        seq = [(self.core, self.core_add)]
+        seq = [self.core]
         for axis in path:
             if axis == "z":
-                for k in range(1, LINE):
-                    seq.append((functools.partial(self.z_copies, path=path, k=k, back=False), functools.partial(self.z_add, path=path, k=k)))
+                seq += [functools.partial(self.line, path=path, k=k) for k in range(1, LINE)]
             else:
-                seq.append((functools.partial(self.pair_send, path=path, axis=axis), functools.partial(self.pair_add, path=path, axis=axis)))
+                seq.append(functools.partial(self.pair, path=path, axis=axis))
         for axis in path[::-1]:
             if axis == "z":
-                for k in range(1, LINE):
-                    seq.append((functools.partial(self.z_copies, path=path, k=k, back=True), None))
+                seq += [functools.partial(self.line_back, path=path, k=k) for k in range(1, LINE)]
             else:
-                seq.append((functools.partial(self.pair_back, path=path, axis=axis), None))
-        seq.append((self.core_back, None))
-        return seq
+                seq.append(functools.partial(self.pair_back, path=path, axis=axis))
+        return seq + [self.core_back]
 
     def run_stage(self, f, s, path):
         seq = self.steps(path)
         if s > 0:
-            copies, add = seq[s - 1]
-            for cp in copies(f):
-                if isinstance(cp, tuple):
-                    sends, gets, one = cp
-                    pl.when(sends)(one.wait_send)
-                    pl.when(gets)(one.wait_recv)
+            for sends, gets, cp, then in seq[s - 1](f):
+                if sends is None:
+                    cp.wait()
+                    if then is not None:
+                        then()
+                    continue
+                pl.when(sends)(cp.wait_send)
+
+                @pl.when(gets)
+                def _():
+                    cp.wait_recv()
+                    if then is not None:
+                        then()
+        if s < len(seq):
+            for sends, gets, cp, then in seq[s](f):
+                if sends is None:
+                    cp.start()
                 else:
-                    cp.wait()
-            if add is not None:
-                add(f)
-        if s < len(seq):
-            for cp in seq[s][0](f):
-                if isinstance(cp, tuple):
-                    pl.when(cp[0])(cp[2].start)
-                else:
-                    cp.start()
-
-    def stages(self, path):
-        return len(self.steps(path)) + 1
-
-    def step(self, i, last, paths, skew):
-        n = self.stages(paths[0])
+                    pl.when(sends)(cp.start)
+
+    def step(self, i, last, paths, offsets):
+        n = len(offsets)
         for s in range(n - 1, -1, -1):
-            f = i - s * skew
+            f = i - offsets[s]
 
             def go(f=f, s=s):
                 if s in (0, n - 1):
-                    self.run_stage(f, s, paths[0])
+                    self.run_stage(f, s, "xzy")
                     return
-                for core, path in enumerate(paths):
-                    @pl.when(self.p.c == core)
+                for path, takes in paths(self.p.c, f):
+                    @pl.when(takes)
                     def _():
                         self.run_stage(f, s, path)
             pl.when((f >= 0) & (f < last))(go)
 
 
-PATHS = ("xzy", "yzx")
-SKEW = 2
+STAGES = 2 * (2 + LINE) + 1
+
+
+def paths(core, f):
+    return [("xzy", core == 0), ("yzx", core == 1)]
+
+
+OFFSETS = [0, 1] + [2 * s - 1 for s in range(2, STAGES - 1)] + [2 * STAGES - 4]
+CORE_SLOTS = 4
+T_OFFSETS = [0, 1, 3, 4, 6, 7, 9, 10, 12, 13, 15]
 CHUNK = 256
 SMALL = 16
 
@@ -253,7 +247,7 @@
         self.imgs = self.slots // 4
         self.qh = x_hi.shape[1]
         self.p, self.ph = 4 * self.q, 4 * self.qh
-        self.ks = w_tok1_lo.shape[1]
+        self.ks = w_tok1_lo.shape[0]
         self.k = 4 * self.ks
         self.ff = w_chan_in.shape[1]
         self.chunks = self.ff // CHUNK
@@ -261,18 +255,16 @@
         self.own = 2 * self.qh
         self.hi0 = self.imgs * self.pr
         self.rows = self.hi0 + self.own
-        self.wl, self.wh = up128(self.p), up128(self.ph)
-        self.lanes = 2 * self.wl + 2 * self.wh + 256
         self.half_rows = CHUNK * (self.d // 256)
-        self.t_lo = 3 * self.own
-        self.t_rows = -(-(self.t_lo + self.k) // (16 * SHARDS)) * (16 * SHARDS)
+        self.hb = -(-self.ph // 256)
+        self.blocks = 2 + 2 * self.hb
 
 
 def kernel(
     S,
-    x_lo, x_hi, cot_lo, cot_hi, counts, wpack, bias_lo, bias_hi, w_in, w_out, b_in, b_out, gain1, shift1, gain2, shift2,
+    x_lo, x_hi, cot_lo, cot_hi, counts, w1l, b1l, w2l, b2l, w1h, b1h, w2h, b2h, w_in, w_out, b_in, b_out, gain1, shift1, gain2, shift2,
     out_lo, out_hi, grad_lo, grad_hi, g_sum, t_sum, s_sum,
-    xl, xh, cl, ch, wg, bl, bh, w2t_lo, w1_lo, w2t_hi, w1_hi, bcol, af, nb, nh, n2, ct, tmp, gmh, hid, gp, winv, woutv,
+    xl, xh, cl, ch, wg, bl, bho, bh, w2t_lo, w1_lo, w2t_hi, w1_hi, bcol, bcols, brow, af, nb, nh, n2, ct, tmp, gmh, hid, gp, winv, woutv,
     g, g_core, g_land, t, t_core, t_land, gw1, gw2, gb, sv, s1, s2,
     lo_send, lo_recv, hi_send, hi_recv, w_send, w_recv, ring_send, ring_recv, g_send, g_recv, t_send, t_recv,
     s_send, s_recv, local, g_kept, t_kept,
@@ -373,18 +365,34 @@
             pl.when(jnp.logical_not(mine))(remote.wait_recv)
 
     my = (1 - y) * 2 + c
-    w_own = pltpu.make_async_copy(wpack, wg.at[m], local.at[4, 0])
-    w_y = rcopy(wpack, wg.at[m], w_send.at[0], w_recv.at[0], dev(1 - y, c))
-    w_c = rcopy(wpack, wg.at[m], w_send.at[1], w_recv.at[1], dev(y, 1 - c))
+
+    def across(v, lanes):
+        n = v.shape[0]
+        return jnp.broadcast_to(v[...].astype(f32).reshape(1, n), (lanes, n)).T.astype(bf16)
+
+    start_hi(hi_out(0, x_hi, xh))
+    wg[m] = jnp.zeros((S.blocks, S.ks, 256), bf16)
+    wg[m, 0, :, 128:256] = across(b1l, 128)
+    wg[m, 1 + S.hb, :, 128:256] = across(b1h, 128)
+    wg[m, 0, :, 0:S.pr] = jnp.zeros((S.ks, S.pr), bf16)
+    wg[m, 0, :, 0:S.p] = w1l[...]
+    wg[m, 1, :, 0:S.p] = w2l[...]
+    for j in range(S.hb):
+        n = min(256, S.ph - 256 * j)
+        wg[m, 2 + j, :, 0:n] = w1h[:, 256 * j:256 * j + n]
+        wg[m, 2 + S.hb + j, :, 0:n] = w2h[:, 256 * j:256 * j + n]
+    w_y = rcopy(wg.at[m, dpi], wg.at[m, dpi], w_send.at[0], w_recv.at[0], dev(1 - y, c))
+    w_y_in = rcopy(wg.at[my, dpi], wg.at[my, dpi], w_send.at[0], w_recv.at[0], dev(1 - y, c))
+    w_c = rcopy(wg.at[m], wg.at[m], w_send.at[1], w_recv.at[1], dev(y, 1 - c))
     w_f = rcopy(wg.at[my], wg.at[my], w_send.at[2], w_recv.at[2], dev(y, 1 - c))
-    w_own.start()
+    w_d = [rcopy(wg.at[my, dpi], wg.at[my, dpi], w_send.at[6 + k], w_recv.at[7 + dpi], dp_dev(k)) for k in range(1, LINE * PAIR)]
     w_y.start()
     w_c.start()
-    start_hi(hi_out(0, x_hi, xh))
-    bias_out = [rcopy(bias_lo, bl.at[m], w_send.at[3 + j], w_recv.at[3 + m], dev(yy, cc)) for j, (yy, cc) in enumerate(peers)]
+    bl[m] = across(b2l, 128)
+    bias_out = [rcopy(bl.at[m], bl.at[m], w_send.at[3 + j], w_recv.at[3 + m], dev(yy, cc)) for j, (yy, cc) in enumerate(peers)]
     start(bias_out)
-    bl[m] = bias_lo[...]
-    bias_hi_out = hi_out(4, bias_hi, bh)
+    bho[...] = across(b2h, 128)
+    bias_hi_out = hi_out(4, bho, bh)
     start_hi(bias_hi_out)
     for i in range(S.imgs):
         start(lo_out(0, i, x_lo, xl))
@@ -398,8 +406,12 @@
     load_in.start()
     load_out.start()
 
-    gv1, sv1 = gain1[...].astype(f32), shift1[...].astype(f32)
-    gv2, sv2 = gain2[...].astype(f32), shift2[...].astype(f32)
+    def line_of(v):
+        return v[...].astype(f32).reshape(1, v.shape[0])
+
+    gv1, sv1 = line_of(gain1), line_of(shift1)
+    gv2, sv2 = line_of(gain2), line_of(shift2)
+    brow[...] = line_of(b_in)
     hi = pl.ds(S.hi0, S.own)
     own = pl.ds(pl.multiple_of(c * S.own, 16), S.own)
 
@@ -432,35 +444,50 @@
     nh_copy = rcopy(nh.at[own], nh.at[own], ring_send.at[0], ring_recv.at[0], dev(y, 1 - c))
     nh_copy.start()
 
-    w_own.wait()
-    w_y.wait()
+    w_y.wait_send()
+    w_y_in.wait_recv()
+    start(w_d)
+    for k in range(1, LINE * PAIR):
+        i = (dpi + k) % (LINE * PAIR)
+        w_d[k - 1].wait_send()
+        rcopy(wg.at[my, i], wg.at[my, i], w_send.at[6 + k], w_recv.at[7 + i], dp_dev(k)).wait_recv()
     w_f.start()
     w_c.wait()
-    w_f.wait()
-    o1, o2, o3, o4 = S.wl, 2 * S.wl, 2 * S.wl + S.wh, 2 * S.wl + 2 * S.wh
+    w_f.wait_send()
+    w_far = rcopy(wg.at[(1 - y) * 2 + 1 - c], wg.at[(1 - y) * 2 + 1 - c], w_send.at[2], w_recv.at[2], dev(y, 1 - c))
+    w_far.wait_recv()
+
+    def block(b, n):
+        return wg[:, b, :, 0:n].reshape(S.k, n)
 
     def w1t_lo():
-        return wg[:, :, 0:S.pr].reshape(S.k, S.pr)
+        return block(0, S.pr)
 
     def w2_lo():
-        return wg[:, :, o1:o1 + S.pr].reshape(S.k, S.pr)
-
-    def w1t_hi():
-        return wg[:, :, o2:o2 + S.ph].reshape(S.k, S.ph)
-
-    def w2_hi():
-        return wg[:, :, o3:o3 + S.ph].reshape(S.k, S.ph)
+        return block(1, S.pr)
+
+    def bias_of(b):
+        return wg[:, b, :, 128:256].reshape(S.k, 128).astype(f32)[:, 127:128]
+
+    spans = [(256 * j, min(256, S.ph - 256 * j)) for j in range(S.hb)]
+
+    def mm_hi(first, rows_of):
+        return functools.reduce(jnp.add, [mm(block(first + j, n), rows_of[at:at + n, :]) for j, (at, n) in enumerate(spans)])
+
+    for k in range(2):
+        bcols[k] = jnp.broadcast_to(bias_of(k * (1 + S.hb)), (S.k, 128))
 
     def b1_lo():
-        return wg[:, :, o4:o4 + 128].reshape(S.k, 128).astype(f32)[:, 0:1]
+        return bcols[0, :, 0:1]
 
     def b1_hi():
-        return wg[:, :, o4 + 128:o4 + 256].reshape(S.k, 128).astype(f32)[:, 0:1]
+        return bcols[1, :, 0:1]
 
     w1_lo[...] = w1t_lo().T
     w2t_lo[...] = w2_lo().T
-    w1_hi[...] = w1t_hi().T
-    w2t_hi[...] = w2_hi().T
+    for j, (at, n) in enumerate(spans):
+        w1_hi[at:at + n, :] = block(2 + j, n).T
+        w2t_hi[at:at + n, :] = block(2 + S.hb + j, n).T
     for j, (yy, cc) in enumerate(peers):
         bias_out[j].wait_send()
         s = yy * 2 + cc
@@ -486,7 +513,7 @@
 
     lax.fori_loop(0, S.imgs, fwd_lo, 0)
     nh_copy.wait()
-    ht = gelu(mm(w1t_hi(), nh[...]) + b1_hi()).astype(bf16)
+    ht = gelu(mm_hi(2, nh) + b1_hi()).astype(bf16)
     bcol_hi = bh[...].reshape(S.own, 128).astype(f32)[:, 0:1]
     af[hi, :] = af[hi, :] + (mm(w2t_hi[own, :], ht) + bcol_hi)
 
@@ -528,7 +555,7 @@
 
     def channel(f):
         cols = pl.ds(pl.multiple_of(f * CHUNK, CHUNK), CHUNK)
-        h, slope = gelu_both(mm(n2[...], winv[:, cols]) + b_in[:, cols].astype(f32))
+        h, slope = gelu_both(mm(n2[...], winv[:, cols]) + brow[:, cols])
         hb = h.astype(bf16)
         hid[:, cols] = hb
         gpre = (mm(ct[...], woutv[cols, :], 1, 1) * slope).astype(bf16)
@@ -539,7 +566,7 @@
         for j in range(d // 256):
             g[f, S.half_rows + CHUNK * j:S.half_rows + CHUNK * (j + 1), :] = grad[:, 256 * j:256 * (j + 1)].astype(bf16)
 
-    bo = b_out[...].astype(f32)
+    bo = line_of(b_out)
 
     def channel_back(rows, live):
         a = af[rows, :]
@@ -598,12 +625,11 @@
         gm_copy.wait()
         n = nb[hi, :]
         gm = n2[hi, :]
-        h, slope = gelu_both(mm(w1t_hi(), nh[...]) + b1_hi())
-        ga2 = mm(gm, h.astype(bf16), 1, 1)
-        gpt = (mm(w2_hi(), gmh[...]) * slope).astype(bf16)
-        ga1 = mm(n, gpt, 1, 1)
-        once = jnp.where(c == 0, 1.0, 0.0).astype(f32)
-        sv[11:12, 0:S.k] += mm(ones, gpt, 1, 1)[0:1] * once
+        h, slope = gelu_both(mm_hi(2, nh) + b1_hi())
+        ga2 = mm(h.astype(bf16), gmh[...], 1, 1) * 0.5
+        gpt = (mm_hi(2 + S.hb, gmh) * slope).astype(bf16)
+        ga1 = mm(gpt, nh[...], 1, 1) * 0.5
+        sv[11:12, 0:S.k] += mm(ones, gpt, 1, 1)[0:1] * 0.5
         sv[pl.ds(12 + c, 1), 0:S.own] = mm(ones, gm, 1, 1)[0:1]
         gn = mm(w1_hi[own, :], gpt)
         grad = first_norm_back(xh[...].reshape(S.own, d).astype(f32), gn, hi)
@@ -611,24 +637,27 @@
         start_hi(hi_back(3, xh, grad_hi))
         for j in range(S.ff // d):
             sv[5 + j:6 + j, :] = gb[:, d * j:d * (j + 1)]
-        for k in range(2):
-            @pl.when(c == k)
-            def _():
-                t[0, S.t_rows * k:S.t_rows * k + S.own, :] = ga1[:, 0:256].astype(bf16)
-                t[0, S.t_rows * k + S.own:S.t_rows * k + 2 * S.own, :] = ga2[:, 0:256].astype(bf16)
-                t[0, S.t_rows * k + 2 * S.own:S.t_rows * k + 3 * S.own, 0:128] = ga1[:, 256:384].astype(bf16)
-                t[0, S.t_rows * k + 2 * S.own:S.t_rows * k + 3 * S.own, 128:256] = ga2[:, 256:384].astype(bf16)
-        t[0, S.t_lo:S.t_lo + S.k, :] = gw1[...].astype(bf16)
-        t[0, S.t_rows + S.t_lo:S.t_rows + S.t_lo + S.k, :] = gw2[...].astype(bf16)
         s1[m] = sv[...]
         start(s1_out)
+        for ks in range(4):
+            k0, yy, cc = ks * S.ks, ks // 2, ks % 2
+
+            def put(j, v, n=256):
+                row = (cc * SHARDS + 2 * j + yy) * S.ks
+                t[0, row:row + S.ks, 0:n] = v.astype(bf16)
+
+            put(0, gw1[k0:k0 + S.ks, :])
+            put(1, gw2[k0:k0 + S.ks, :])
+            for j in range(S.hb):
+                n = min(256, S.ph - 256 * j)
+                put(2 + j, ga1[k0:k0 + S.ks, 256 * j:256 * j + n], n)
+                put(2 + S.hb + j, ga2[k0:k0 + S.ks, 256 * j:256 * j + n], n)
 
     s1_out = [rcopy(s1.at[m], s1.at[m], s_send.at[j], s_recv.at[m], dev(yy, cc)) for j, (yy, cc) in enumerate(peers)]
     s2_out = [rcopy(s2.at[dpi], s2.at[dpi], s_send.at[3 + k], s_recv.at[4 + dpi], dp_dev(k)) for k in range(1, LINE * PAIR)]
 
     ar = AllReduce(p, g, g_core, g_land, g_sum, g_send, g_recv, g_kept)
-    art = AllReduce(p, t, t_core, t_land, t_sum, t_send, t_recv, t_kept)
-    stages = ar.stages(PATHS[0])
+    art = TokenSum(p, t, t_core, t_land, t_sum, t_send, t_recv, t_kept)
     nc = S.chunks
     b0 = nc + 1 + S.imgs
     t0 = b0 + S.imgs
@@ -639,18 +668,20 @@
         pl.when((i > nc) & (i < b0))(lambda: back_lo(i - nc - 1))
         pl.when((i >= b0) & (i < t0))(lambda: token_lo(i - b0))
         pl.when(i == t0)(token_hi)
-        ar.step(i, nc, PATHS, SKEW)
-        art.step(i - t0, 1, PATHS, 1)
+        pl.when(i == t0 + 2)(small_sums)
+        ar.step(i, nc, paths, OFFSETS)
+        art.step(i - t0, T_OFFSETS)
         return carry
 
-    lax.fori_loop(0, max(nc + (stages - 1) * SKEW, t0 + stages), step, 0)
-
-    for j, (yy, cc) in enumerate(peers):
-        s = yy * 2 + cc
-        s1_out[j].wait_send()
-        rcopy(s1.at[s], s1.at[s], s_send.at[j], s_recv.at[s], dev(yy, cc)).wait_recv()
-    s2[dpi] = s1[0] + s1[1] + s1[2] + s1[3]
-    start(s2_out)
+    def small_sums():
+        for j, (yy, cc) in enumerate(peers):
+            s = yy * 2 + cc
+            s1_out[j].wait_send()
+            rcopy(s1.at[s], s1.at[s], s_send.at[j], s_recv.at[s], dev(yy, cc)).wait_recv()
+        s2[dpi] = s1[0] + s1[1] + s1[2] + s1[3]
+        start(s2_out)
+
+    lax.fori_loop(0, max(nc + OFFSETS[-1], t0 + 1 + T_OFFSETS[-1]), step, 0)
     for k in range(1, LINE * PAIR):
         i = (dpi + k) % (LINE * PAIR)
         s2_out[k - 1].wait_send()
@@ -679,51 +710,121 @@
     d, dma = S.d, pltpu.SemaphoreType.DMA
     nc = S.chunks
     unit = 2 * S.half_rows // (2 * SHARDS)
-    tu = S.t_rows // SHARDS
     scratch = [
         pltpu.VMEM((4, S.imgs, S.q, d), bf16), pltpu.VMEM((2, S.qh, d), bf16),
         pltpu.VMEM((4, S.imgs, S.q, d), bf16), pltpu.VMEM((2, S.qh, d), bf16),
-        pltpu.VMEM((4, S.ks, S.lanes), bf16), pltpu.VMEM((4, S.q, 128), bf16), pltpu.VMEM((2, S.qh, 128), bf16),
+        pltpu.VMEM((4, S.blocks, S.ks, 256), bf16), pltpu.VMEM((4, S.q, 128), bf16), pltpu.VMEM((S.qh, 128), bf16), pltpu.VMEM((2, S.qh, 128), bf16),
         pltpu.VMEM((S.pr, S.k), bf16), pltpu.VMEM((S.pr, S.k), bf16), pltpu.VMEM((S.ph, S.k), bf16), pltpu.VMEM((S.ph, S.k), bf16),
-        pltpu.VMEM((S.pr, 128), f32),
+        pltpu.VMEM((S.pr, 128), f32), pltpu.VMEM((2, S.k, 128), f32), pltpu.VMEM((1, S.ff), f32),
         pltpu.VMEM((S.rows, d), f32), pltpu.VMEM((S.rows, d), bf16), pltpu.VMEM((S.ph, d), bf16), pltpu.VMEM((S.rows, d), bf16),
         pltpu.VMEM((S.rows, d), bf16), pltpu.VMEM((S.pr, d), f32), pltpu.VMEM((S.ph, d), bf16),
         pltpu.VMEM((S.rows, S.ff), bf16), pltpu.VMEM((S.rows, S.ff), bf16), pltpu.VMEM((d, S.ff), bf16), pltpu.VMEM((S.ff, d), bf16),
-        pltpu.VMEM((nc, 2 * SHARDS * unit, 256), bf16), pltpu.VMEM((2 * SKEW, SHARDS * unit, 256), bf16), pltpu.VMEM((nc, LANDED * unit, 256), bf16),
-        pltpu.VMEM((1, 2 * S.t_rows, 256), bf16), pltpu.VMEM((1, S.t_rows, 256), bf16), pltpu.VMEM((1, LANDED * tu, 256), bf16),
+        pltpu.VMEM((nc, 2 * SHARDS * unit, 256), bf16), pltpu.VMEM((CORE_SLOTS, SHARDS * unit, 256), bf16), pltpu.VMEM((nc, LANDED * unit, 256), bf16),
+        pltpu.VMEM((1, 2 * SHARDS * S.ks, 256), bf16), pltpu.VMEM((1, SHARDS * S.ks, 256), bf16), pltpu.VMEM((1, LANDED * S.ks, 256), bf16),
         pltpu.VMEM((S.k, 256), f32), pltpu.VMEM((S.k, 256), f32), pltpu.VMEM((1, S.ff), f32),
         pltpu.VMEM((SMALL, d), f32), pltpu.VMEM((4, SMALL, d), f32), pltpu.VMEM((LINE * PAIR, SMALL, d), f32),
-        dma((4, 3, S.imgs)), dma((4, 4, S.imgs)), dma((5, 2)), dma((5, 2)), dma((6,)), dma((7,)), dma((2,)), dma((2,)),
+        dma((4, 3, S.imgs)), dma((4, 4, S.imgs)), dma((5, 2)), dma((5, 2)), dma((14,)), dma((15,)), dma((2,)), dma((2,)),
         dma((nc, NSEM)), dma((nc, NSEM)), dma((1, NSEM)), dma((1, NSEM)), dma((11,)), dma((12,)), dma((5, S.imgs + 1)), dma((nc,)), dma((1,)),
     ]
     return pl.pallas_call(
         functools.partial(kernel, S),
         out_shape=(
             sds((S.slots, S.q, d), bf16), sds((2, S.qh, d), bf16), sds((S.slots, S.q, d), bf16), sds((2, S.qh, d), bf16),
-            sds((nc, 2 * S.half_rows, 256), bf16), sds((1, 2 * S.t_rows, 256), bf16), sds((SMALL, d), f32),
+            sds((nc, 2 * S.half_rows, 256), bf16), sds((1, S.blocks * S.ks, 256), bf16), sds((SMALL, d), f32),
         ),
-        in_specs=[A, A, A, A, M, A, V, V, A, A, V, V, V, V, V, V],
+        in_specs=[A, A, A, A, M] + [V] * 8 + [A, A] + [V] * 6,
         out_specs=(A, A, A, A, A, A, V),
         scratch_shapes=scratch,
         compiler_params=pltpu.CompilerParams(collective_id=0, has_side_effects=True, vmem_limit_bytes=63 * 1024 * 1024),
     )(*args)
 
 
-def widen(S, g):
+class TokenSum(AllReduce):
+    def part(self, i):
+        return self.out.at[0, self.sh(i, 1)]
+
+    def line_back(self, f, path, k):
+        z, base = self.p.z, self.p.x * LINE
+        inside = lambda p: self.part(base + jnp.clip(p, 0, LINE - 1))
+        up, down = inside(z + 1 - k), inside(z + k - 1)
+        up_src, down_src, more = up, down, []
+        if k == 1:
+            up_src = down_src = self.half(f, (base + z) * PAIR + self.p.y, 1)
+            more = [(None, None, pltpu.make_async_copy(up_src, up, self.kept.at[f]), None)]
+        return [((z < LINE - 1) & (z >= k - 1), (z > 0) & (z >= k), self.copy(f, UP_BACK + k, up_src, up, self.p.up()), None),
+                ((z > 0) & (z <= LINE - k), (z < LINE - 1) & (z <= LINE - 1 - k), self.copy(f, DOWN_BACK + k, down_src, down, self.p.down()), None)] + more
+
+    def x_back(self, f):
+        ref = self.out.at[0, self.sh(self.p.x * LINE, LINE)]
+        return [(None, None, self.copy(f, X_BACK, ref, ref, self.p.pair("x")), None)]
+
+    def steps(self, path):
+        there = super().steps(path)[:2 + LINE]
+        return there + [functools.partial(self.line_back, path=path, k=k) for k in range(1, LINE)] + [self.x_back]
+
+    def step(self, i, offsets):
+        for s in range(len(offsets)):
+            pl.when(i == offsets[s])(functools.partial(self.run_stage, 0, s, "xzy"))
+
+
+def finish(S, out_lo, out_hi, grad_lo, grad_hi, g, t, s):
     d = S.d
-
-    def place(g_ref, in_ref, out_ref):
-        in_ref[...] = g_ref[0, 0:d, :].astype(f32)
+    sds = jax.ShapeDtypeStruct
+
+    def place(ol, oh, gl, gh, g_ref, t_ref, s_ref, *outs):
+        (o_lo, o_hi, r_lo, r_hi, l1g, l1b, w1l, b1l, w2l, b2l, w1h, b1h, w2h, b2h, l2g, l2b, w_in, b_in, w_out, b_out) = outs
+        m = lax.axis_index("mp")
+        w_in[...] = g_ref[0, 0:d, :].astype(f32)
         for j in range(d // 256):
-            out_ref[:, 256 * j:256 * (j + 1)] = g_ref[0, S.half_rows + CHUNK * j:S.half_rows + CHUNK * (j + 1), :].astype(f32)
-
+            w_out[:, 256 * j:256 * (j + 1)] = g_ref[0, S.half_rows + CHUNK * j:S.half_rows + CHUNK * (j + 1), :].astype(f32)
+        o_lo[...] = ol[...]
+        r_lo[...] = gl[...].astype(f32)
+
+        @pl.when(pl.program_id(0) == 0)
+        def _():
+            o_hi[...] = oh[...]
+            r_hi[...] = gh[...].astype(f32)
+            w1l[...] = t_ref[0, :, 0:S.p].astype(f32)
+            w2l[...] = t_ref[1, :, 0:S.p].astype(f32)
+            for j in range(S.hb):
+                n = min(256, S.ph - 256 * j)
+                w1h[:, 256 * j:256 * j + n] = t_ref[2 + j, :, 0:n].astype(f32)
+                w2h[:, 256 * j:256 * j + n] = t_ref[2 + S.hb + j, :, 0:n].astype(f32)
+            for i, o in ((0, b_out), (1, l2g), (2, l2b), (3, l1g), (4, l1b)):
+                o[...] = s_ref[i, :]
+            for j in range(S.ff // d):
+                b_in[d * j:d * (j + 1)] = s_ref[5 + j, :]
+            for j in range(4):
+                @pl.when(m == j)
+                def _():
+                    b1l[...] = s_ref[9, S.ks * j:S.ks * (j + 1)]
+                    b2l[...] = s_ref[10, S.q * j:S.q * (j + 1)]
+                    b1h[...] = s_ref[11, S.ks * j:S.ks * (j + 1)]
+                    b2h[...] = s_ref[12 + j // 2, S.qh * (j % 2):S.qh * (j % 2 + 1)]
+
+    def whole(v):
+        return pl.BlockSpec(v.shape, lambda i: (0,) * len(v.shape))
+
+    image = pl.BlockSpec((S.slots // S.chunks, S.q, d), lambda i: (i, 0, 0))
+    vec = lambda n: sds((n,), f32)
+    shapes = [
+        sds(out_lo.shape, bf16), sds(out_hi.shape, bf16), sds(out_lo.shape, f32), sds(out_hi.shape, f32), vec(d), vec(d),
+        sds((S.ks, S.p), f32), vec(S.ks), sds((S.ks, S.p), f32), vec(S.q), sds((S.ks, S.ph), f32), vec(S.ks), sds((S.ks, S.ph), f32), vec(S.qh),
+        vec(d), vec(d), sds((d, S.ff), f32), vec(S.ff), sds((S.ff, d), f32), vec(d),
+    ]
+    outs = [whole(v) for v in shapes]
+    outs[0] = outs[2] = image
+    outs[16] = pl.BlockSpec((d, CHUNK), lambda i: (0, i))
+    outs[18] = pl.BlockSpec((CHUNK, d), lambda i: (i, 0))
+    t = t.reshape(S.blocks, S.ks, 256)
     return pl.pallas_call(
         place,
         grid=(S.chunks,),
-        out_shape=(jax.ShapeDtypeStruct((d, S.ff), f32), jax.ShapeDtypeStruct((S.ff, d), f32)),
-        in_specs=[pl.BlockSpec((1, 2 * S.half_rows, 256), lambda i: (i, 0, 0))],
-        out_specs=(pl.BlockSpec((d, CHUNK), lambda i: (0, i)), pl.BlockSpec((CHUNK, d), lambda i: (i, 0))),
-    )(g)
+        out_shape=shapes,
+        in_specs=[image, whole(out_hi), image, whole(grad_hi), pl.BlockSpec((1, 2 * S.half_rows, 256), lambda i: (i, 0, 0)), whole(t), whole(s)],
+        out_specs=outs,
+        compiler_params=pltpu.CompilerParams(vmem_limit_bytes=63 * 1024 * 1024),
+    )(out_lo, out_hi, grad_lo, grad_hi, g, t, s)
 
 
 def body(
@@ -731,44 +832,18 @@
     x_lo, x_hi, cot_lo, cot_hi, counts, ln1_gain, ln1_bias, w_tok1_lo, b_tok1_lo, w_tok2_lo, b_tok2_lo, w_tok1_hi, b_tok1_hi,
     w_tok2_hi, b_tok2_hi, ln2_gain, ln2_bias, w_chan_in, b_chan_in, w_chan_out, b_chan_out,
 ):
-    S = Sizes(x_lo, x_hi, w_tok1_lo, w_chan_in)
-
-    def lanes(w, n):
-        return jnp.pad(w, ((0, 0), (0, n - w.shape[1])))
-
-    def column(b):
-        return jnp.broadcast_to(b[:, None], (b.shape[0], 128))
-
-    wpack = jnp.concatenate(
-        [lanes(w_tok1_lo.T, S.wl), lanes(w_tok2_lo, S.wl), lanes(w_tok1_hi.T, S.wh), lanes(w_tok2_hi, S.wh), column(b_tok1_lo), column(b_tok1_hi)],
-        axis=1,
-    )
-    row = lambda v: v[None, :]
+    w1_lo, w1_hi = w_tok1_lo.T, w_tok1_hi.T
+    S = Sizes(x_lo, x_hi, w1_lo, w_chan_in)
     out_lo, out_hi, grad_lo, grad_hi, g, t, s = mixer(
         S,
-        (x_lo, x_hi, cot_lo, cot_hi, counts, wpack, column(b_tok2_lo), column(b_tok2_hi), w_chan_in, w_chan_out, row(b_chan_in), row(b_chan_out),
-         row(ln1_gain), row(ln1_bias), row(ln2_gain), row(ln2_bias)),
+        (x_lo, x_hi, cot_lo, cot_hi, counts, w1_lo, b_tok1_lo, w_tok2_lo, b_tok2_lo, w1_hi, b_tok1_hi, w_tok2_hi, b_tok2_hi,
+         w_chan_in, w_chan_out, b_chan_in, b_chan_out, ln1_gain, ln1_bias, ln2_gain, ln2_bias),
     )
-    g_in, g_out = widen(S, g)
-    t = t.astype(f32).reshape(2, S.t_rows, 256)
     if groups is not None:
-        g_in, g_out, t, s = lax.psum((g_in, g_out, t, s), "dp", axis_index_groups=groups)
-    m = lax.axis_index("mp")
-    ks = m * S.ks
-    lo1 = lax.dynamic_slice(t[0], (S.t_lo + ks, 0), (S.ks, 256))[:, :S.p].T
-    lo2 = lax.dynamic_slice(t[1], (S.t_lo + ks, 0), (S.ks, 256))[:, :S.p]
-    n = S.own
-    hi1 = jnp.concatenate([t[:, 0:n], t[:, 2 * n:3 * n, 0:128]], axis=2).reshape(2 * n, 384)
-    hi2 = jnp.concatenate([t[:, n:2 * n], t[:, 2 * n:3 * n, 128:256]], axis=2).reshape(2 * n, 384)
-    hi1 = lax.dynamic_slice(hi1, (0, ks), (S.ph, S.ks))
-    hi2 = lax.dynamic_slice(hi2, (0, ks), (S.ph, S.ks)).T
-    b2_hi = jnp.concatenate([s[12, :n], s[13, :n]])
-    cut = lambda v, w: lax.dynamic_slice(v, (m * w,), (w,))
-    return (
-        out_lo, out_hi, grad_lo.astype(f32), grad_hi.astype(f32), s[3], s[4],
-        lo1, cut(s[9], S.ks), lo2, cut(s[10], S.q), hi1, cut(s[11], S.ks), hi2, cut(b2_hi, S.qh),
-        s[1], s[2], g_in, s[5:9].reshape(S.ff), g_out, s[0],
-    )
+        g, t, s = lax.psum((g.astype(f32), t.astype(f32), s), "dp", axis_index_groups=groups)
+    res = list(finish(S, out_lo, out_hi, grad_lo, grad_hi, g, t, s))
+    res[6], res[10] = res[6].T, res[10].T
+    return tuple(res)
 
 
 def solution(mesh):

time: 241 us -> 192 us (0.80)
  local copies, waits for them, and re-layouts: 23.7 us -> 0 us
  Pallas kernels: 211 us -> 191 us
  other arithmetic: 4.14 us -> 0 us
    pallas_call x1, Pallas kernels: 199 us -> 175 us  [mixer(): pl.pallas_call(functools.partial(kernel, S), out_shape=(sds((S.slots, S.q...]
    broadcast_in_dim x8 -> x0, local copies, waits for them, and re-layouts: 10.3 us -> none  [the longest x6 7.61 us: body(): row = lambda v: v[None, :]]
    unnamed x23 -> x0, local copies, waits for them, and re-layouts: 7.67 us -> none
    convert_element_type x3 -> x0, other arithmetic: 3.94 us -> none  [the longest x1 1.52 us: body(): t = t.astype(f32).reshape(2, S.t_rows, 256)]
    pallas_call x1, Pallas kernels: 12.6 us -> 15.5 us  [finish(): pl.pallas_call(place, grid=(S.chunks,), out_shape=shapes, in_specs=[image...]
    dynamic_slice x5 -> x0, local copies, waits for them, and re-layouts: 2.61 us -> none  [the longest x3 1.8 us: body(): cut = lambda v, w: lax.dynamic_slice(v, (m * w,), (w,))]
where the time goes in v2:
time: 192 us; the launch traced here: 191 us
  Pallas kernels  191 us (99%)
    pallas_call x1, Pallas kernels, mixer(): pl.pallas_call(functools.partial(kernel, S), out_shape=(sds((S.slots, S.q...  175 us
    pallas_call x1, Pallas kernels, finish(): pl.pallas_call(place, grid=(S.chunks,), out_shape=shapes, in_specs=[image...  15.5 us

profile of v2, /device:TPU:0, one launch (start us, length us, event | category | flops | bytes accessed | tf_op | source)
XLA Modules:
  0.0 191.5 jit_solution(12798100397218017028)
XLA Ops:
  0.7 175.1 %shard_map.356 = (bf16[12,49,768]{2,1,0:T(8,128)(2,1)}, bf16[2,144,768]{2,1,0:T(8,128)(2,1)}, bf16[12,49,768]{2,1,0:T(8,128)(2,1)}, bf16[2,144,768]{2,1,0:T(8,12...) custom-call(bf16[12,49,768]{2,1,0:T(8,128)(2,1)} %x_lo.1, ...), custom_call_target="tpu_custom_call" | custom-call | tf_op jit(solution)/shard_map/pallas_call | solution.py:729
  175.8 15.5 %shard_map.357 = (bf16[12,49,768]{2,1,0:T(8,128)(2,1)}, bf16[2,144,768]{2,1,0:T(8,128)(2,1)}, f32[12,49,768]{2,1,0:T(8,128)}, f32[2,144,768]{2,1,0:T(8,128)}, f3...) custom-call(bf16[12,49,768]{2,1,0:T(8,128)(2,1)} %get-tuple-element., ...), custom_call_target="tpu_custom_call" | custom-call | tf_op jit(solution)/shard_map/pallas_call | solution.py:820

commit v3 on v2

--- a/solution.py
+++ b/solution.py
@@ -585,7 +585,6 @@
     def back_hi():
         out = channel_back(hi, live_hi)
         ch[...] = out.astype(bf16).reshape(2, S.qh, d)
-        start_hi(hi_back(2, ch, out_hi))
         gmh[own, :] = n2[hi, :]
         gm_copy.start()
 
@@ -594,8 +593,6 @@
     def back_lo(i):
         tmp[...] = channel_back(img(i), live_lo(i))
         scatter_rows(cl, i)
-        start(lo_back(2, i, cl, out_lo))
-        lo_back_local(2, i, cl, out_lo).start()
 
     ones = jnp.ones((8, d), bf16)
 
@@ -662,6 +659,10 @@
     b0 = nc + 1 + S.imgs
     t0 = b0 + S.imgs
 
+    def send_out(k):
+        start(lo_back(2, k, cl, out_lo))
+        lo_back_local(2, k, cl, out_lo).start()
+
     def step(i, carry):
         pl.when(i < nc)(lambda: channel(i))
         pl.when(i == nc)(back_hi)
@@ -669,6 +670,9 @@
         pl.when((i >= b0) & (i < t0))(lambda: token_lo(i - b0))
         pl.when(i == t0)(token_hi)
         pl.when(i == t0 + 2)(small_sums)
+        pl.when(i == t0 + 2)(lambda: start_hi(hi_back(2, ch, out_hi)))
+        for k in range(S.imgs):
+            pl.when(i == t0 + 4 + 2 * k)(functools.partial(send_out, k))
         ar.step(i, nc, paths, OFFSETS)
         art.step(i - t0, T_OFFSETS)
         return carry

time: 192 us -> 189 us (0.984)
  Pallas kernels: 191 us -> 188 us
    pallas_call x1, Pallas kernels: 175 us -> 172 us  [mixer(): pl.pallas_call(functools.partial(kernel, S), out_shape=(sds((S.slots, S.q...]
where the time goes in v3:
time: 189 us; the launch traced here: 188 us
  Pallas kernels  188 us (99%)
    pallas_call x1, Pallas kernels, mixer(): pl.pallas_call(functools.partial(kernel, S), out_shape=(sds((S.slots, S.q...  172 us
    pallas_call x1, Pallas kernels, finish(): pl.pallas_call(place, grid=(S.chunks,), out_shape=shapes, in_specs=[image...  15.5 us

profile of v3, /device:TPU:0, one launch (start us, length us, event | category | flops | bytes accessed | tf_op | source)
XLA Modules:
  0.0 188.5 jit_solution(18314223463338200002)
XLA Ops:
  0.7 172.1 %shard_map.356 = (bf16[12,49,768]{2,1,0:T(8,128)(2,1)}, bf16[2,144,768]{2,1,0:T(8,128)(2,1)}, bf16[12,49,768]{2,1,0:T(8,128)(2,1)}, bf16[2,144,768]{2,1,0:T(8,12...) custom-call(bf16[12,49,768]{2,1,0:T(8,128)(2,1)} %x_lo.1, ...), custom_call_target="tpu_custom_call" | custom-call | tf_op jit(solution)/shard_map/pallas_call | solution.py:733
  172.8 15.5 %shard_map.357 = (bf16[12,49,768]{2,1,0:T(8,128)(2,1)}, bf16[2,144,768]{2,1,0:T(8,128)(2,1)}, f32[12,49,768]{2,1,0:T(8,128)}, f32[2,144,768]{2,1,0:T(8,128)}, f3...) custom-call(bf16[12,49,768]{2,1,0:T(8,128)(2,1)} %get-tuple-element., ...), custom_call_target="tpu_custom_call" | custom-call | tf_op jit(solution)/shard_map/pallas_call | solution.py:824

commit v4 on v3

--- a/solution.py
+++ b/solution.py
@@ -176,7 +176,7 @@
 
     def step(self, i, last, paths, offsets):
         n = len(offsets)
-        for s in range(n - 1, -1, -1):
+        for s in range(n):
             f = i - offsets[s]
 
             def go(f=f, s=s):
@@ -774,13 +774,16 @@
 def finish(S, out_lo, out_hi, grad_lo, grad_hi, g, t, s):
     d = S.d
     sds = jax.ShapeDtypeStruct
+    per = 2
 
     def place(ol, oh, gl, gh, g_ref, t_ref, s_ref, *outs):
         (o_lo, o_hi, r_lo, r_hi, l1g, l1b, w1l, b1l, w2l, b2l, w1h, b1h, w2h, b2h, l2g, l2b, w_in, b_in, w_out, b_out) = outs
         m = lax.axis_index("mp")
-        w_in[...] = g_ref[0, 0:d, :].astype(f32)
-        for j in range(d // 256):
-            w_out[:, 256 * j:256 * (j + 1)] = g_ref[0, S.half_rows + CHUNK * j:S.half_rows + CHUNK * (j + 1), :].astype(f32)
+        for k in range(per):
+            at = slice(CHUNK * k, CHUNK * (k + 1))
+            w_in[:, at] = g_ref[k, 0:d, :].astype(f32)
+            for j in range(d // 256):
+                w_out[at, 256 * j:256 * (j + 1)] = g_ref[k, S.half_rows + CHUNK * j:S.half_rows + CHUNK * (j + 1), :].astype(f32)
         o_lo[...] = ol[...]
         r_lo[...] = gl[...].astype(f32)
 
@@ -809,7 +812,7 @@
     def whole(v):
         return pl.BlockSpec(v.shape, lambda i: (0,) * len(v.shape))
 
-    image = pl.BlockSpec((S.slots // S.chunks, S.q, d), lambda i: (i, 0, 0))
+    image = pl.BlockSpec((per * S.slots // S.chunks, S.q, d), lambda i: (i, 0, 0))
     vec = lambda n: sds((n,), f32)
     shapes = [
         sds(out_lo.shape, bf16), sds(out_hi.shape, bf16), sds(out_lo.shape, f32), sds(out_hi.shape, f32), vec(d), vec(d),
@@ -818,14 +821,14 @@
     ]
     outs = [whole(v) for v in shapes]
     outs[0] = outs[2] = image
-    outs[16] = pl.BlockSpec((d, CHUNK), lambda i: (0, i))
-    outs[18] = pl.BlockSpec((CHUNK, d), lambda i: (i, 0))
+    outs[16] = pl.BlockSpec((d, per * CHUNK), lambda i: (0, i))
+    outs[18] = pl.BlockSpec((per * CHUNK, d), lambda i: (i, 0))
     t = t.reshape(S.blocks, S.ks, 256)
     return pl.pallas_call(
         place,
-        grid=(S.chunks,),
+        grid=(S.chunks // per,),
         out_shape=shapes,
-        in_specs=[image, whole(out_hi), image, whole(grad_hi), pl.BlockSpec((1, 2 * S.half_rows, 256), lambda i: (i, 0, 0)), whole(t), whole(s)],
+        in_specs=[image, whole(out_hi), image, whole(grad_hi), pl.BlockSpec((per, 2 * S.half_rows, 256), lambda i: (i, 0, 0)), whole(t), whole(s)],
         out_specs=outs,
         compiler_params=pltpu.CompilerParams(vmem_limit_bytes=63 * 1024 * 1024),
     )(out_lo, out_hi, grad_lo, grad_hi, g, t, s)

time: 189 us -> 187 us (0.989)
  Pallas kernels: 188 us -> 186 us
where the time goes in v4:
time: 187 us
  Pallas kernels  186 us (99%)
    pallas_call x1, Pallas kernels, mixer(): pl.pallas_call(functools.partial(kernel, S), out_shape=(sds((S.slots, S.q...  172 us
    pallas_call x1, Pallas kernels, finish(): pl.pallas_call(place, grid=(S.chunks // per,), out_shape=shapes, in_specs...  14.3 us

profile of v4, /device:TPU:0, one launch (start us, length us, event | category | flops | bytes accessed | tf_op | source)
XLA Modules:
  0.0 186.7 jit_solution(13478272807768995383)
XLA Ops:
  0.7 171.6 %shard_map.356 = (bf16[12,49,768]{2,1,0:T(8,128)(2,1)}, bf16[2,144,768]{2,1,0:T(8,128)(2,1)}, bf16[12,49,768]{2,1,0:T(8,128)(2,1)}, bf16[2,144,768]{2,1,0:T(8,12...) custom-call(bf16[12,49,768]{2,1,0:T(8,128)(2,1)} %x_lo.1, ...), custom_call_target="tpu_custom_call" | custom-call | tf_op jit(solution)/shard_map/pallas_call | solution.py:733
  172.2 14.3 %shard_map.357 = (bf16[12,49,768]{2,1,0:T(8,128)(2,1)}, bf16[2,144,768]{2,1,0:T(8,128)(2,1)}, f32[12,49,768]{2,1,0:T(8,128)}, f32[2,144,768]{2,1,0:T(8,128)}, f3...) custom-call(bf16[12,49,768]{2,1,0:T(8,128)(2,1)} %get-tuple-element., ...), custom_call_target="tpu_custom_call" | custom-call | tf_op jit(solution)/shard_map/pallas_call | solution.py:827
